TPU v7x, 128 devices: a whole 4x4x4 slice. The times are simulated.
128 devices in a mesh: grp: 4 (over x_hi, core), dev: 32 (over z, y, x_lo).
Axes of the slice: x: 4 (x_hi: 2, x_lo: 2; x = x_hi * 2 + x_lo), y: 4, z: 4, core: 2. Of those that a mesh axis runs over, the one named last changes fastest.
Arguments:
- spin_config: int32 [256, 144], P(('grp', 'dev')), may hold values from -1 to 1, as said below
- layer_acts: bfloat16 [256, 36, 768], P(('grp', 'dev'))
- cotangent: bfloat16 [256, 36, 768], P(('grp', 'dev'))
- patch_embed: bfloat16 [4, 768], replicated, may hold values from -3 to 3
- energies: float32 [256], P(('grp', 'dev')), may hold values from -0.24 to 0.24
- slot_sample: int32 [256], replicated, may hold values from 0 to 255, each once
- damping: float32 [], replicated, may hold values from 0.0001 to 0.0002
Outputs:
- update: float32 [589824], P(('grp', 'dev'))
Inputs may be any that keep to these rules, and one draw needn't show every extreme that they name: `spin_config`: each entry is -1 or +1; the sites of patch t are entries 4 t to 4 t + 3.
All inputs are finite; a program needn't handle non-finite values.
Results may differ from a plain program's by a relative error of at most 0.001.
The roundings to bfloat16 on the way count: a program that leaves them out, or rounds other values in their place, can miss the bound.
Values may be sent and summed in bfloat16 or wider, within the bound.
A program may use at most 64 MiB of HBM per device.

v0:
```python
import math

import jax
import jax.numpy as jnp
from jax import lax
from jax.sharding import PartitionSpec as P


def solve_system(system, target):
    factor = jnp.linalg.cholesky(system)
    forward = lax.linalg.triangular_solve(factor, target[:, None], left_side=True, lower=True)
    backward = lax.linalg.triangular_solve(
        factor, forward, left_side=True, lower=True, transpose_a=True
    )
    return backward[:, 0]


def shards(spin_config, layer_acts, cotangent, patch_embed, energies, slot_sample, damping):
    local_count = layer_acts.shape[0]
    token_count = layer_acts.shape[1]
    model_width = layer_acts.shape[2]
    patches = spin_config.reshape(local_count, token_count, -1).astype(jnp.float32)
    embedded = jnp.einsum("stk,kd->std", patches, patch_embed.astype(jnp.float32))
    layer_in = (layer_acts.astype(jnp.float32) + embedded).astype(jnp.bfloat16)
    row_float = jnp.einsum("sti,stj->sij", layer_in, cotangent, preferred_element_type=jnp.float32)
    row_local = (
        (row_float * (1.0 / math.sqrt(token_count)))
        .astype(jnp.bfloat16)
        .reshape(local_count, model_width * model_width)
    )
    local_rows = lax.all_to_all(row_local, ("grp", "dev"), split_axis=1, concat_axis=0, tiled=True)
    sample_total = local_rows.shape[0]
    param_total = model_width * model_width
    column_float = local_rows.astype(jnp.float32)
    centered = (
        (column_float - jnp.mean(column_float, axis=0, keepdims=True))
        * (1.0 / math.sqrt(param_total))
    ).astype(jnp.bfloat16)
    partial_gram = lax.dot_general(
        centered, centered, (((1,), (1,)), ((), ())), preferred_element_type=jnp.float32
    )
    gram_matrix = lax.psum(partial_gram, ("grp", "dev"))
    all_energy = lax.all_gather(energies, ("grp", "dev"), axis=0, tiled=True)
    shifted = jnp.take(all_energy, slot_sample) - jnp.mean(all_energy)
    system = gram_matrix + damping * jnp.eye(sample_total, dtype=jnp.float32)
    weights = solve_system(system, shifted)
    step_scale = -math.sqrt(param_total / sample_total)
    return step_scale * jnp.dot(
        weights, centered.astype(jnp.float32), precision=lax.Precision.HIGHEST
    )


def solution(mesh):
    return jax.shard_map(
        shards,
        mesh=mesh,
        in_specs=(
            P(("grp", "dev"), None),
            P(("grp", "dev"), None, None),
            P(("grp", "dev"), None, None),
            P(),
            P(("grp", "dev")),
            P(),
            P(),
        ),
        out_specs=P(("grp", "dev")),
        check_vma=False,
    )
```

profile of v0, /device:TPU:1, one launch (start us, length us, event | category | flops | bytes accessed | tf_op | source)
XLA Modules:
  0.0 340.3 jit_solution(8518412686171092533)
XLA Ops:
  6.5 0.7 convert_element_type.38
  7.3 0.1 convert_element_type.39
  7.4 0.8 fusion.17
  8.2 1.1 fusion.8
  9.3 0.8 multiply_convert_fusion
  10.1 3.4 all_to_all.10
  13.5 5.5 %copy.18 = bf16[2,128,4608]{2,0,1:T(2,128)(2,1)} copy(bf16[2,128,4608]{2,1,0:T(8,128)(2,1)} %all_to_all.10) | data formatting | bytes 4718592 | tf_op jit(solution)/shard_map/all_to_all | solution.py:31
  19.0 11.5 %all-to-all-start = ((bf16[2,128,4608]{2,0,1:T(2,128)(2,1)}), bf16[2,128,4608]{2,0,1:T(2,128)(2,1)S(1)}, u32[]{:S(2)}, u32[]{:S(2)}) async-start(bf16[2,128,4608]{2,0,1:T(2,128)(2,1)} %copy.18), calls=%async_computation | async-start | bytes 4718592 | tf_op jit(solution)/shard_map/all_to_all | solution.py:31
  30.5 0.0 all-reduce.4.cloned.1.call-start
  30.6 0.2 dynamic-update-slice.11
  30.8 84.4 %all-reduce.1 = f32[256]{0:T(256)S(1)} all-reduce(f32[256]{0:T(256)S(1)} %dynamic-update-slice.11), channel_id=1, replica_groups=mesh['grp'=4,'dev'=32] {'grp','dev'}, use_global_device_ids=true, to_apply=%add.1 | all-reduce | flops 256 | bytes 2048
  115.2 0.6 reduce_sum.19
  115.8 1.9 gather_fusion
  118.4 1.9 convert_reduce_fusion
  120.3 3.9 %fusion.2 = bf16[128,2,4608]{2,1,0:T(2,128)(2,1)} fusion(bf16[2,128,4608]{2,0,1:T(2,128)(2,1)S(1)} %all-to-all-done, f32[4608]{0:T(1024)S(1)} %broadcast_multiply_fusion.1), kind=kLoop, calls=%fused_computation.8 | loop fusion | flops 4718592 | bytes 4737024 | tf_op jit(solution)/shard_map/convert_element_type | solution.py:38
  124.2 3.0 convert_element_type.45
  127.3 1.5 fusion.28
  128.8 0.0 all-reduce.4.cloned.1.call-update
  129.5 138.5 %all-reduce.4.cloned.1.call-done = f32[256,256]{0,1:T(8,128)} async-done(((f32[256,256]{0,1:T(8,128)}), f32[256,256]{0,1:T(8,128)}) %all-reduce.4.cloned.1.call-update) | async-done | bytes 262160 | tf_op jit(solution)/shard_map/psum | solution.py:42
  268.0 1.0 select_add_fusion
  269.0 0.1 copy.20
  269.1 1.0 fusion.7
  270.1 11.7 %cholesky.49 = f32[128,128]{1,0:T(8,128)S(1)} custom-call(f32[128,128]{1,0:T(8,128)S(1)} %cholesky.115), custom_call_target="Cholesky" | custom-call | tf_op jit(solution)/shard_map/jit(cholesky)/cholesky | solution.py:10
  281.9 9.8 %custom-call.16 = f32[1,128,128]{1,2,0:T(8,128)S(1)} custom-call(f32[1,128,128]{2,1,0:T(8,128)S(1)} %get-tuple-element.32), custom_call_target="InvertDiagBlocksLowerTriangular" | custom-call | tf_op jit(solution)/shard_map/jit(cholesky)/cholesky | solution.py:10
  291.7 0.2 fusion.11
  291.9 0.3 convolution_subtract_fusion
  292.2 11.7 %cholesky.103 = f32[128,128]{1,0:T(8,128)S(1)} custom-call(f32[128,128]{1,0:T(8,128)S(1)} %convolution_subtract_fusion), custom_call_target="Cholesky" | custom-call | tf_op jit(solution)/shard_map/jit(cholesky)/cholesky | solution.py:10
  303.9 0.1 copy.23
  304.0 0.1 copy.22
  304.1 0.1 copy.21
  304.3 0.7 compare_reduce_fusion
  306.3 0.1 triangular_solve.75
  306.4 4.3 %while.1 = (s32[]{:T(128)}, f32[256,256]{0,1:T(8,128)S(1)}, s32[2,2]{1,0:T(2,128)S(1)}, f32[2,128,128]{2,1,0:T(8,128)S(1)}, s32[]{:T(128)}) while((s32[]{:T(128)}, f32[256,256]{0,1:T(8,128)S(1)}, s32[2,2]{1,0:T(2,128)S(1)}, f32[2,128,128]{2,1,0:T(8,128)S(1)}, s32[]{:T(128)}) %tuple.23), condition=%wide.while_cond, body=%wide.while_body.sunk | while | flops 2 | bytes 393321 | solution.py:12
  306.4 0.7 fusion.40
  307.1 1.3 dynamic-slice.7
  308.4 0.1 copy.36
  308.5 0.7 fusion.40
  309.2 1.3 dynamic-slice.7
  310.5 0.1 copy.36
  310.7 19.9 %custom-call.17 = f32[2,128,128]{1,2,0:T(8,128)S(1)} custom-call(f32[2,128,128]{2,1,0:T(8,128)S(1)} %get-tuple-element.12), custom_call_target="InvertDiagBlocksLowerTriangular" | custom-call | tf_op jit(solution)/shard_map/triangular_solve | solution.py:12
  330.6 0.2 fusion.14
  330.7 0.2 fusion.6
  330.9 0.2 convolution_bitcast_fusion.3
  331.1 0.2 convolution_bitcast_fusion.2
  331.3 0.2 fusion.4
  331.5 0.2 convolution_bitcast_fusion
  331.7 1.1 convolution_reduce_fusion
  332.8 0.6 broadcast_multiply_fusion
  (25 shorter events, 0.2 us)
Async XLA Ops:
  6.5 2.8 copy-start
  19.0 11.6 %copy-start.2 = (f32[2]{0:T(128)S(1)}, f32[2]{0:T(128)}, u32[]{:S(2)}) copy-start(f32[2]{0:T(128)} %param.11) | copy-start | bytes 28
  19.0 96.8 %copy-start.1 = (s32[256]{0:T(256)S(1)}, s32[256]{0:T(256)}, u32[]{:S(2)}) copy-start(s32[256]{0:T(256)} %param.12) | copy-start | bytes 3076
  19.0 99.4 %all-to-all-start = ((bf16[2,128,4608]{2,0,1:T(2,128)(2,1)}), bf16[2,128,4608]{2,0,1:T(2,128)(2,1)S(1)}, u32[]{:S(2)}, u32[]{:S(2)}) async-start(bf16[2,128,4608]{2,0,1:T(2,128)(2,1)} %copy.18), calls=%async_computation | async-start | bytes 4718592 | tf_op jit(solution)/shard_map/all_to_all | solution.py:31
  30.5 237.5 %all-reduce.4.cloned.1.call-start = ((), (), s32[]{:S(2)}) async-start(), calls=%async_computation.1 | async-start | bytes 524288 | tf_op jit(solution)/shard_map/psum | solution.py:42
Sparse Core Ops, SparseCore 0:
  128.9 139.0 all-reduce.3
where the time goes:
time: 341 us; the launch traced here: 340 us
  waiting for transfers between devices  139 us (41%)
  blocking collectives  84.4 us (25%)
  other arithmetic  64.7 us (19%)
  local copies, waits for them, and re-layouts  19 us (6%)
  between operations  16.2 us (5%)
  starting transfers between devices  11.5 us (3%)
  matrix products  5.88 us (2%)
    psum x1, waiting for transfers between devices, shards(): gram_matrix = lax.psum(partial_gram, ('grp', 'dev'))  139 us
    unnamed x1, blocking collectives  84.4 us
    another operation x6, other arithmetic, solve_system(): factor = jnp.linalg.cholesky(system)  34 us
    another operation x3, other arithmetic, solve_system(): lax.linalg.triangular_solve(factor, forward, left_side=True, lower=True,...  19.9 us
    all_to_all x1, starting transfers between devices, shards(): lax.all_to_all(row_local, ('grp', 'dev'), split_axis=1, concat_axis=0, ti...  11.5 us
    all_to_all x2, local copies, waits for them, and re-layouts, shards(): lax.all_to_all(row_local, ('grp', 'dev'), split_axis=1, concat_axis=0, ti...  8.86 us
  transfers between devices with their start and end apart: 2, of which 1 were waited for; matrix products, arithmetic and copies ran while one was open for 1% of the time, Pallas kernels for 0%

commit v1 on v0

v1 whole, which is shorter than its diff:
```python
import math

import jax
import jax.numpy as jnp
from jax import lax
from jax.experimental import pallas as pl
from jax.experimental.pallas import tpu as pltpu
from jax.sharding import PartitionSpec as P

F32 = jnp.float32
BF = jnp.bfloat16
MESH = pl.DeviceIdType.MESH
SLOTS = 256
WIDTH = 768
TOKS = 36
IB = 48
JB = 96
ROWS2 = 2 * TOKS
LANES = 128


def flip(index, high):
    return index + high * (1 - 2 * (index % 2))


def place():
    g = lax.axis_index("grp")
    d = lax.axis_index("dev")
    x_hi, core = g // 2, g % 2
    z, rb = d // 8, d % 8
    return g, d, x_hi, core, z, rb


def column_device(a, b):
    g, z = a // 4, a % 4
    return (g, z * 8 + flip(b, g // 2))


def remote(src, dst, send_sem, recv_sem, device):
    return pltpu.make_async_remote_copy(
        src_ref=src, dst_ref=dst, send_sem=send_sem, recv_sem=recv_sem,
        device_id=device, device_id_type=MESH,
    )


def gram_kernel(energy_ref, lin_ref, cin_ref, slot_ref, out_ref, cen_ref,
                lall, call, rbuf, gacc, gp, rr, ssum, cr, tile, s2,
                l1s, l1r, c1s, c1r, c2s, c2r, c3s, c3r, l2s, l2r,
                rs_s, rs_r, cs_s, cs_r, bc_s, bc_r, ag_s, ag_r):
    g, d, x_hi, core, z, rb = place()
    a = g * 4 + z
    b = flip(rb, x_hi)
    chip = x_hi * 4 + z
    partner = (x_hi * 2 + 1 - core, d)

    barrier = pltpu.get_barrier_semaphore()
    for k in range(1, 16):
        pl.semaphore_signal(barrier, inc=1, device_id=column_device((a + k) % 16, b), device_id_type=MESH)
    for k in range(1, 8):
        pl.semaphore_signal(barrier, inc=1, device_id=column_device(a, (b + k) % 8), device_id_type=MESH)
    pl.semaphore_wait(barrier, 22)

    sends = []

    def start(copy):
        copy.start()
        sends.append(copy)

    for k in range(1, 8):
        bt = (b + k) % 8
        start(remote(cin_ref.at[bt], call.at[a, b], c1s.at[k], c1r.at[b], column_device(a, bt)))
    for k in range(1, 16):
        at = (a + k) % 16
        start(remote(lin_ref.at[at], lall.at[b, a], l1s.at[k], l1r.at[a], column_device(at, b)))
    call[a, b] = cin_ref[b]
    lall[b, a] = lin_ref[a]

    for k in range(1, 8):
        bs = (b + 8 - k) % 8
        remote(call.at[a, bs], call.at[a, bs], c1s.at[k], c1r.at[bs], partner).wait_recv()
    for k in range(1, 8):
        ct = (chip + k) % 8
        at = (ct // 4) * 8 + core * 4 + ct % 4
        start(remote(call.at[a], call.at[a], c2s.at[k], c2r.at[chip], column_device(at, b)))
    start(remote(call.at[a], call.at[a], c3s.at[0], c3r.at[chip], partner))

    for k in range(1, 16):
        asrc = (a + 16 - k) % 16
        remote(lall.at[b, asrc], lall.at[b, asrc], l1s.at[k], l1r.at[asrc], partner).wait_recv()
    for k in range(1, 8):
        bt = (b + k) % 8
        start(remote(lall.at[b], lall.at[b], l2s.at[k], l2r.at[b], column_device(a, bt)))

    for k in range(1, 8):
        cs = (chip + 8 - k) % 8
        asrc = (cs // 4) * 8 + core * 4 + cs % 4
        remote(call.at[asrc], call.at[asrc], c2s.at[k], c2r.at[cs], partner).wait_recv()
        start(remote(call.at[asrc], call.at[asrc], c3s.at[k], c3r.at[cs], partner))
    for k in range(0, 8):
        cs = (chip + 8 - k) % 8
        asrc = (cs // 4) * 8 + (1 - core) * 4 + cs % 4
        remote(call.at[asrc], call.at[asrc], c3s.at[k], c3r.at[cs], partner).wait_recv()
    for k in range(1, 8):
        bs = (b + 8 - k) % 8
        remote(lall.at[bs], lall.at[bs], l2s.at[k], l2r.at[bs], partner).wait_recv()

    lane = lax.broadcasted_iota(jnp.int32, (IB, LANES), 1)
    first = jnp.where(lane < TOKS, 1.0, 0.0).astype(BF)
    second = jnp.where((lane >= TOKS) & (lane < ROWS2), 1.0, 0.0).astype(BF)

    def rows_step(asrc, carry):
        high = asrc // 8
        for bs in range(8):
            left = lall[bs, asrc]
            left = jnp.concatenate([left * first, left * second], axis=0)
            prod = lax.dot_general(left[:, :ROWS2], call[asrc, bs], (((1,), (0,)), ((), ())),
                                   preferred_element_type=F32)
            at = asrc * 8 + flip(bs, high)
            rbuf[pl.ds(pl.multiple_of(at * 2 * IB, 2 * IB), 2 * IB), :] = (
                prod * (1.0 / math.sqrt(TOKS))).astype(BF).astype(F32)
        return carry

    lax.fori_loop(0, 16, rows_step, 0)

    gacc[...] = jnp.zeros_like(gacc)
    inv_root = 1.0 / math.sqrt(WIDTH * WIDTH)

    def gram_step(step, carry):
        parts = []
        for u in range(4):
            i = step * 4 + u
            x = rbuf[pl.ds(i, SLOTS, stride=IB), :]
            mean = jnp.sum(x, axis=0, keepdims=True) * (1.0 / SLOTS)
            c = ((x - mean) * inv_root).astype(BF)
            cen_ref[i] = c
            parts.append(c)
        c = jnp.concatenate(parts, axis=1)
        gacc[...] += lax.dot_general(c, c, (((1,), (1,)), ((), ())), preferred_element_type=F32)
        return carry

    lax.fori_loop(0, IB // 4, gram_step, 0)

    for t in range(48):
        blk, w = t // 16, t % 16
        r0 = (0, 128, 128)[blk] + 8 * w
        c0 = (0, 0, 128)[blk]
        gp[t // 6, t % 6] = gacc[r0:r0 + 8, c0:c0 + 128]
    slots = slot_ref[...]
    base = (g * 32 + d) * 2
    mine = jnp.where(slots == base, energy_ref[0, 0], 0.0) + jnp.where(slots == base + 1, energy_ref[0, 1], 0.0)
    for r in range(8):
        gp[r, 6] = mine if r == 0 else jnp.zeros_like(mine)

    for k in range(1, 8):
        bt = (b + k) % 8
        start(remote(gp.at[bt], rr.at[b], rs_s.at[k], rs_r.at[b], column_device(a, bt)))
    for k in range(1, 8):
        bs = (b + 8 - k) % 8
        remote(rr.at[bs], rr.at[bs], rs_s.at[k], rs_r.at[bs], partner).wait_recv()
    rr[b] = gp[b]
    total = rr[0]
    for k in range(1, 8):
        total = total + rr[k]
    ssum[...] = total

    for j in range(7):
        owner = (j % 2) * 8 + j // 2

        @pl.when(a != owner)
        def _():
            remote(ssum.at[j], cr.at[a], cs_s.at[j], cs_r.at[a], column_device(owner + 0 * a, b)).start()

    for j in range(7):
        owner = (j % 2) * 8 + j // 2

        @pl.when(a == owner)
        def _():
            for k in range(1, 16):
                asrc = (a + k) % 16
                remote(cr.at[asrc], cr.at[asrc], cs_s.at[j], cs_r.at[asrc], partner).wait_recv()
            cr[owner] = ssum[j]
            t = cr[0]
            for k in range(1, 16):
                t = t + cr[k]
            s2[j] = t
            for k in range(1, 16):
                at = (a + k) % 16
                remote(s2.at[j], s2.at[j], bc_s.at[k], bc_r.at[j], column_device(at, b)).start()

    for j in range(7):
        owner = (j % 2) * 8 + j // 2

        @pl.when(a != owner)
        def _():
            remote(ssum.at[j], cr.at[a], cs_s.at[j], cs_r.at[a], partner).wait_send()
            remote(s2.at[j], s2.at[j], bc_s.at[0], bc_r.at[j], partner).wait_recv()

    for k in range(1, 8):
        bt = (b + k) % 8
        start(remote(s2, out_ref.at[b], ag_s.at[k], ag_r.at[b], column_device(a, bt)))
    out_ref[b] = s2[...]
    for k in range(1, 8):
        bs = (b + 8 - k) % 8
        remote(out_ref.at[bs], out_ref.at[bs], ag_s.at[k], ag_r.at[bs], partner).wait_recv()

    for copy in sends:
        copy.wait_send()
    for j in range(7):
        owner = (j % 2) * 8 + j // 2

        @pl.when(a == owner)
        def _():
            for k in range(1, 16):
                remote(s2.at[j], s2.at[j], bc_s.at[k], bc_r.at[j], partner).wait_send()


def gram_call(energy, lin, cin, slots):
    dma = pltpu.SemaphoreType.DMA
    vmem = pl.BlockSpec(memory_space=pltpu.VMEM)
    return pl.pallas_call(
        gram_kernel,
        out_shape=(
            jax.ShapeDtypeStruct((8, 7, 8, LANES), F32),
            jax.ShapeDtypeStruct((IB, SLOTS, LANES), BF),
        ),
        in_specs=[pl.BlockSpec(memory_space=pltpu.SMEM), vmem, vmem, vmem],
        out_specs=(vmem, vmem),
        scratch_shapes=[
            pltpu.VMEM((8, 16, IB, LANES), BF),
            pltpu.VMEM((16, 8, ROWS2, LANES), BF),
            pltpu.VMEM((SLOTS * IB, LANES), F32),
            pltpu.VMEM((SLOTS, SLOTS), F32),
            pltpu.VMEM((8, 7, 8, LANES), F32),
            pltpu.VMEM((8, 7, 8, LANES), F32),
            pltpu.VMEM((7, 8, LANES), F32),
            pltpu.VMEM((16, 8, LANES), F32),
            pltpu.VMEM((8, LANES), F32),
            pltpu.VMEM((7, 8, LANES), F32),
            dma((16,)), dma((16,)), dma((8,)), dma((8,)), dma((8,)), dma((8,)),
            dma((8,)), dma((8,)), dma((8,)), dma((8,)),
            dma((8,)), dma((8,)), dma((8,)), dma((16,)), dma((16,)), dma((8,)), dma((8,)), dma((8,)),
        ],
        compiler_params=pltpu.CompilerParams(
            collective_id=0, has_side_effects=True, vmem_limit_bytes=48 * 1024 * 1024),
        name="gram",
    )(energy, lin, cin, slots)


def split3(x):
    high = x.astype(BF)
    rest = x - high.astype(F32)
    mid = rest.astype(BF)
    return high, mid, (rest - mid.astype(F32)).astype(BF)


def solve_kernel(damp_ref, gt_ref, w_ref, W):
    n, B = SLOTS, 8
    for t in range(48):
        blk, w = t // 16, t % 16
        r0 = (0, 128, 128)[blk] + 8 * w
        c0 = (0, 0, 128)[blk]
        W[r0:r0 + 8, c0:c0 + 128] = gt_ref[t // 6, t % 6]
    W[0:128, 128:256] = W[128:256, 0:128].T
    energy = gt_ref[0, 6]
    e_row = jnp.concatenate([energy[0:1, :], energy[1:2, :]], axis=1)
    sh = e_row - jnp.sum(e_row, axis=1, keepdims=True) * (1.0 / n)
    rows = lax.broadcasted_iota(jnp.int32, (n, n), 0)
    cols = lax.broadcasted_iota(jnp.int32, (n, n), 1)
    eye = rows == cols
    W[:, 0:n] = W[:, 0:n] + jnp.where(eye, damp_ref[0, 0], 0.0)
    W[:, n:] = jnp.broadcast_to(jnp.sum(jnp.where(eye, sh, 0.0), axis=1, keepdims=True), (n, LANES))

    lane128 = lax.broadcasted_iota(jnp.int32, (B, LANES), 1)
    sub128 = lax.broadcasted_iota(jnp.int32, (B, LANES), 0)
    laneN = lax.broadcasted_iota(jnp.int32, (B, n + LANES), 1)
    subN = lax.broadcasted_iota(jnp.int32, (B, n + LANES), 0)

    def chain(k, p):
        dd = pltpu.roll(p[:, 0:n], n - B * k, 1)[:, 0:LANES]
        dd = jnp.where(lane128 < B, dd, jnp.where(lane128 == sub128 + B, 1.0, 0.0))
        for i in range(B):
            c = jnp.broadcast_to(dd[:, i:i + 1], (B, LANES))
            inv = 1.0 / c[i:i + 1, :]
            cm = jnp.where(sub128 == i, 0.0, c)
            r_d = dd[i:i + 1, :] * inv
            dd = jnp.where(sub128 == i, r_d, dd - cm * r_d)
            r_p = p[i:i + 1, :] * jnp.concatenate([inv] * 3, axis=1)
            p = jnp.where(subN == i, r_p, p - jnp.concatenate([cm] * 3, axis=1) * r_p)
        dinv = jnp.concatenate([dd, jnp.zeros((B, n - LANES), F32)], axis=1)
        dinv = pltpu.roll(dinv, lax.rem(B * k - B + n, n), 1)
        dinv = jnp.concatenate([dinv, jnp.zeros((B, LANES), F32)], axis=1)
        inside = (laneN >= B * k) & (laneN < B * k + B)
        ident = jnp.where(laneN == B * k + subN, 1.0, 0.0)
        return jnp.where(inside, ident - dinv, p), jnp.where(inside, -dinv, p)

    def stack(p, x):
        ph, pm, pl_ = split3(p)
        xh, xm, xl = split3(x)
        join = lambda *parts: jnp.concatenate([q.astype(F32) for q in parts], axis=0).astype(BF)
        return join(ph, ph, pm, ph, pl_, pm), join(xh, xm, xh, xl, xh, xm)

    def body(k, carry):
        p, p_old, x_old, xs_old = carry
        ps, xs = stack(p_old[:, 0:n], x_old)
        W[...] = W[...] - lax.dot_general(ps, xs, (((0,), (0,)), ((), ())), preferred_element_type=F32)
        kp = pl.multiple_of(jnp.maximum(k - 1, 0) * B, B)
        W[pl.ds(kp, B), :] = jnp.where(k > 0, xs_old, W[pl.ds(kp, B), :])
        x_new, xs_new = chain(k, p)
        kn = pl.multiple_of(jnp.minimum(k + 1, n // B - 1) * B, B)
        nxt = W[pl.ds(kn, B), :]
        col = pltpu.roll(nxt[:, 0:n], n - B * k, 1)
        for i in range(B):
            nxt = nxt - col[:, i:i + 1] * x_new[i:i + 1, :]
        return nxt, p, x_new, xs_new

    zero = jnp.zeros((B, n + LANES), F32)
    _, p_old, x_old, xs_old = lax.fori_loop(0, n // B, body, (W[0:B, :], zero, zero, zero))
    ps, xs = stack(p_old[:, 0:n], x_old)
    w_ref[...] = W[:, n:] - lax.dot_general(ps, xs[:, n:], (((0,), (0,)), ((), ())), preferred_element_type=F32)
    w_ref[n - B:, :] = xs_old[:, n:]


def solve_call(damping, tiles):
    vmem = pl.BlockSpec(memory_space=pltpu.VMEM)
    return pl.pallas_call(
        solve_kernel,
        out_shape=jax.ShapeDtypeStruct((SLOTS, LANES), F32),
        in_specs=[pl.BlockSpec(memory_space=pltpu.SMEM), vmem],
        out_specs=vmem,
        scratch_shapes=[pltpu.VMEM((SLOTS, SLOTS + LANES), F32)],
        name="solve",
    )(damping, tiles)


def update_kernel(w_ref, cen_ref, out_ref, u, send, recv):
    g, d, x_hi, core, z, rb = place()
    a = g * 4 + z
    b = flip(rb, x_hi)
    barrier = pltpu.get_barrier_semaphore()
    for k in range(1, 8):
        pl.semaphore_signal(barrier, inc=1, device_id=column_device(a, (b + k) % 8), device_id_type=MESH)

    scale = -math.sqrt(WIDTH * WIDTH / SLOTS)

    def step(r, carry):
        rows = []
        for v in range(6):
            c = cen_ref[r * 6 + v].astype(F32)
            rows.append(jnp.sum(c * w_ref[...], axis=0, keepdims=True) * scale)
        rows.append(jnp.zeros((2, LANES), F32))
        u[r] = jnp.concatenate(rows, axis=0)
        return carry

    lax.fori_loop(0, 8, step, 0)
    pl.semaphore_wait(barrier, 7)
    sends = []
    for k in range(1, 8):
        rt = (rb + k) % 8
        copy = remote(u.at[rt], out_ref.at[b], send.at[k], recv.at[b], (g, z * 8 + rt))
        copy.start()
        sends.append(copy)
    out_ref[b] = u[rb]
    for k in range(1, 8):
        bs = (b + 8 - k) % 8
        remote(out_ref.at[bs], out_ref.at[bs], send.at[k], recv.at[bs], (g, d)).wait_recv()
    for copy in sends:
        copy.wait_send()


def update_call(weights, cen):
    vmem = pl.BlockSpec(memory_space=pltpu.VMEM)
    return pl.pallas_call(
        update_kernel,
        out_shape=jax.ShapeDtypeStruct((8, 8, LANES), F32),
        in_specs=[vmem, vmem],
        out_specs=vmem,
        scratch_shapes=[pltpu.VMEM((8, 8, LANES), F32), pltpu.SemaphoreType.DMA((8,)), pltpu.SemaphoreType.DMA((8,))],
        compiler_params=pltpu.CompilerParams(
            collective_id=1, has_side_effects=True, vmem_limit_bytes=32 * 1024 * 1024),
        name="update",
    )(weights, cen)


def shards(spin_config, layer_acts, cotangent, patch_embed, energies, slot_sample, damping):
    patches = spin_config.reshape(2, TOKS, -1).astype(F32)
    embedded = jnp.einsum("stk,kd->std", patches, patch_embed.astype(F32))
    layer_in = (layer_acts.astype(F32) + embedded).astype(BF)
    lin = jnp.pad(layer_in.reshape(ROWS2, WIDTH).T, ((0, 0), (0, LANES - ROWS2))).reshape(16, IB, LANES)
    cin = jnp.pad(cotangent.reshape(ROWS2, 8, JB), ((0, 0), (0, 0), (0, LANES - JB))).transpose(1, 0, 2)
    slots = jnp.pad(slot_sample.reshape(2, LANES), ((0, 6), (0, 0)), constant_values=-1)
    tiles, cen = gram_call(energies.reshape(1, 2), lin, cin, slots)
    weights = solve_call(damping.reshape(1, 1), tiles)
    pieces = update_call(weights, cen)
    return pieces[:, :6, :JB].transpose(1, 0, 2).reshape(-1)


def solution(mesh):
    return jax.shard_map(
        shards,
        mesh=mesh,
        in_specs=(
            P(("grp", "dev"), None),
            P(("grp", "dev"), None, None),
            P(("grp", "dev"), None, None),
            P(),
            P(("grp", "dev")),
            P(),
            P(),
        ),
        out_specs=P(("grp", "dev")),
        check_vma=False,
    )
```

time: 341 us -> 105 us (0.31)
  waiting for transfers between devices: 139 us -> 0 us
  Pallas kernels: 0 us -> 95.9 us
  blocking collectives: 84.4 us -> 0 us
  other arithmetic: 64.7 us -> 0.7 us
  between operations: 16.2 us -> 0.76 us
  local copies, waits for them, and re-layouts: 19 us -> 5.09 us
  starting transfers between devices: 11.5 us -> 0 us
  matrix products: 5.88 us -> 1.05 us
    psum x1 -> x0, waiting for transfers between devices: 139 us -> none  [shards(): gram_matrix = lax.psum(partial_gram, ('grp', 'dev'))]
    pallas_call x0 -> x3, Pallas kernels: none -> 95.9 us  [the longest x1 63.5 us: gram_call(): pl.pallas_call(gram_kernel, out_shape=(jax.ShapeDtypeStruct((8, 7, 8, LAN...]
    unnamed x1 -> x0, blocking collectives: 84.4 us -> none
    another operation x9 -> x0, other arithmetic: 54 us -> none  [the longest x6 34 us: solve_system(): factor = jnp.linalg.cholesky(system)]
    all_to_all x1 -> x0, starting transfers between devices: 11.5 us -> none  [shards(): lax.all_to_all(row_local, ('grp', 'dev'), split_axis=1, concat_axis=0, ti...]
    all_to_all x2 -> x0, local copies, waits for them, and re-layouts: 8.86 us -> none  [shards(): lax.all_to_all(row_local, ('grp', 'dev'), split_axis=1, concat_axis=0, ti...]
    convert_element_type x3 -> x1, other arithmetic: 5.63 us -> 0.7 us  [shards(): patches = spin_config.reshape(2, TOKS, -1).astype(F32)]
    another operation x18 -> x0, local copies, waits for them, and re-layouts: 4.61 us -> none
  transfers between devices with their start and end apart: 2 -> 0, of which waited for: 1 -> 0; matrix products, arithmetic and copies ran while one was open for 1% -> 0% of each run, Pallas kernels for 0% -> 0%
where the time goes in v1:
time: 105 us; the launch traced here: 103 us
  Pallas kernels  95.9 us (91%)
  local copies, waits for them, and re-layouts  5.09 us (5%)
  matrix products  1.05 us (1%)
    pallas_call x1, Pallas kernels, gram_call(): pl.pallas_call(gram_kernel, out_shape=(jax.ShapeDtypeStruct((8, 7, 8, LAN...  63.5 us
    pallas_call x1, Pallas kernels, solve_call(): pl.pallas_call(solve_kernel, out_shape=jax.ShapeDtypeStruct((SLOTS, LANES...  27.4 us
    pallas_call x1, Pallas kernels, update_call(): pl.pallas_call(update_kernel, out_shape=jax.ShapeDtypeStruct((8, 8, LANES...  5.07 us
    unnamed x10, local copies, waits for them, and re-layouts  3.31 us

profile of v1, /device:TPU:1, one launch (start us, length us, event | category | flops | bytes accessed | tf_op | source)
XLA Modules:
  0.0 103.5 jit_solution(5167064936139922959)
XLA Ops:
  0.0 0.0 copy-start
  0.0 0.7 convert_element_type.18
  0.7 0.1 convert_element_type.19
  0.8 0.0 copy-done
  0.8 1.1 %fusion = bf16[2,36,768]{2,1,0:T(8,128)(2,1)S(1)} fusion(bf16[2,36,4]{2,1,0:T(8,128)(2,1)S(1)} %convert_element_type.19, bf16[2,36,768]{2,0,1:T(2,128)(2,1)} %param.8, bf16[4,768]{1,0:T(4,128)(2,1)S(1)} %copy-done), kind=kOutput, calls=%fused_computation.1 | convolution fusion | flops 608256 | bytes 227904 | tf_op jit(solution)/shard_map/stk,kd->std/dot_general | solution.py:386
  1.9 0.2 copy.18
  2.1 0.9 copy.14
  3.1 0.2 reshape.27
  3.3 0.7 pad.14.slot_ref
  4.0 0.0 copy-start.3
  4.0 0.7 copy-done.3
  4.6 63.5 %gram.1 = (f32[8,7,8,128]{3,2,1,0:T(8,128)S(1)}, bf16[48,256,128]{2,1,0:T(8,128)(2,1)S(1)}) custom-call(f32[1,2]{1,0:T(1,128)S(1)} %bitcast.15, bf16[16,48,128]{2,1,0:T(8,128)(2,1)S(1)} %bitcast.14, bf16[8,72,128]{2,1,0:T(8,128)(2,1)S(1)} %pad_bitcast_fusion.cin_ref, s32[8,128]{1,0:T(8,128)S(1)} %pad.14.slot_ref), custom_call_target="tpu_custom_call" | custom-call | tf_op jit(solution)/shard_map/gram/pallas_call | solution.py:220
  68.1 0.0 copy-start.2
  68.1 0.7 copy-done.2
  69.4 27.4 %solve.1.w_ref = f32[256,128]{1,0:T(8,128)} custom-call(f32[1,1]{1,0:T(1,128)} %bitcast.13.damp_ref, f32[8,7,8,128]{3,2,1,0:T(8,128)} %copy-done.2), custom_call_target="tpu_custom_call" | custom-call | tf_op jit(solution)/shard_map/solve/pallas_call | solution.py:325
  96.8 0.0 copy-start.1
  96.8 0.9 copy-done.1
  97.7 5.1 %update.1 = f32[8,8,128]{2,1,0:T(8,128)S(1)} custom-call(f32[256,128]{1,0:T(8,128)S(1)} %copy-done.1, bf16[48,256,128]{2,1,0:T(8,128)(2,1)S(1)} %get-tuple-element.8.cen_ref), custom_call_target="tpu_custom_call" | custom-call | tf_op jit(solution)/shard_map/update/pallas_call | solution.py:372
  102.8 0.7 reshape.29
  (6 shorter events, 0.1 us)
Async XLA Ops:
  0.0 0.8 copy-start
  4.0 0.7 copy-start.3
  68.1 0.7 copy-start.2
  96.8 0.9 copy-start.1

commit v2 on v1

--- a/solution.py
+++ b/solution.py
@@ -253,6 +253,76 @@
     return high, mid, (rest - mid.astype(F32)).astype(BF)
 
 
+def recip(x):
+    r = pl.reciprocal(x, approx=True)
+    return r * (2.0 - x * r)
+
+
+def sweep(W, n, B):
+    sub = lax.broadcasted_iota(jnp.int32, (B, LANES), 0)
+    lane = lax.broadcasted_iota(jnp.int32, (B, LANES), 1)
+    masks = [sub == i for i in range(B)]
+    T = n // LANES
+
+    def chain(k, p):
+        t0, l0 = (B * k) // LANES, (B * k) % LANES
+        c = [jnp.broadcast_to(p[t0][:, l0 + j:l0 + j + 1], (B, LANES)) for j in range(B)]
+        p = list(p)
+        for i in range(B):
+            inv = recip(c[i][i:i + 1, :])
+            ci = c[i]
+            for j in range(B):
+                if j == i:
+                    c[j] = jnp.where(masks[i], inv, -ci * inv)
+                else:
+                    t = c[j][i:i + 1, :] * inv
+                    c[j] = jnp.where(masks[i], t, c[j] - ci * t)
+            for v in range(T + 1):
+                r = p[v][i:i + 1, :] * inv
+                p[v] = jnp.where(masks[i], r, p[v] - ci * r)
+        dinv = jnp.zeros((B, LANES), F32)
+        for j in range(B):
+            dinv = jnp.where(lane == l0 + j, c[j], dinv)
+        inside = (lane >= l0) & (lane < l0 + B)
+        ident = jnp.where(lane == l0 + sub, 1.0, 0.0)
+        x, xs = list(p), list(p)
+        x[t0] = jnp.where(inside, ident - dinv, p[t0])
+        xs[t0] = jnp.where(inside, -dinv, p[t0])
+        return x, xs
+
+    def stack(p, x):
+        ph, pm, pl_ = split3(p)
+        xh, xm, xl = split3(x)
+        join = lambda *parts: jnp.concatenate([q.astype(F32) for q in parts], axis=0).astype(BF)
+        return join(ph, ph, pm, ph, pl_, pm), join(xh, xm, xh, xl, xh, xm)
+
+    cat = lambda v: jnp.concatenate(v, axis=1)
+    tn = (((0,), (0,)), ((), ()))
+    p = [W[0:B, v * LANES:(v + 1) * LANES] for v in range(T + 1)]
+    old = None
+    for k in range(n // B):
+        if old is not None:
+            po, xo, xso = old
+            ps, xs = stack(cat(po[:T]), cat(xo))
+            W[...] = W[...] - lax.dot_general(ps, xs, tn, preferred_element_type=F32)
+            W[B * (k - 1):B * k, :] = cat(xso)
+        x, xs = chain(k, p)
+        old = (p, x, xs)
+        if k + 1 < n // B:
+            nxt = [W[B * (k + 1):B * (k + 2), v * LANES:(v + 1) * LANES] for v in range(T + 1)]
+            t0, l0 = (B * k) // LANES, (B * k) % LANES
+            cols = [nxt[t0][:, l0 + i:l0 + i + 1] for i in range(B)]
+            for v in range(T + 1):
+                terms = [cols[i] * x[v][i:i + 1, :] for i in range(B)]
+                while len(terms) > 1:
+                    terms = [terms[q] + terms[q + 1] for q in range(0, len(terms), 2)]
+                nxt[v] = nxt[v] - terms[0]
+            p = nxt
+    po, xo, xso = old
+    ps, xs = stack(cat(po[:T]), xo[T])
+    return W[:, n:] - lax.dot_general(ps, xs, tn, preferred_element_type=F32), xso[T]
+
+
 def solve_kernel(damp_ref, gt_ref, w_ref, W):
     n, B = SLOTS, 8
     for t in range(48):
@@ -269,55 +339,9 @@
     eye = rows == cols
     W[:, 0:n] = W[:, 0:n] + jnp.where(eye, damp_ref[0, 0], 0.0)
     W[:, n:] = jnp.broadcast_to(jnp.sum(jnp.where(eye, sh, 0.0), axis=1, keepdims=True), (n, LANES))
-
-    lane128 = lax.broadcasted_iota(jnp.int32, (B, LANES), 1)
-    sub128 = lax.broadcasted_iota(jnp.int32, (B, LANES), 0)
-    laneN = lax.broadcasted_iota(jnp.int32, (B, n + LANES), 1)
-    subN = lax.broadcasted_iota(jnp.int32, (B, n + LANES), 0)
-
-    def chain(k, p):
-        dd = pltpu.roll(p[:, 0:n], n - B * k, 1)[:, 0:LANES]
-        dd = jnp.where(lane128 < B, dd, jnp.where(lane128 == sub128 + B, 1.0, 0.0))
-        for i in range(B):
-            c = jnp.broadcast_to(dd[:, i:i + 1], (B, LANES))
-            inv = 1.0 / c[i:i + 1, :]
-            cm = jnp.where(sub128 == i, 0.0, c)
-            r_d = dd[i:i + 1, :] * inv
-            dd = jnp.where(sub128 == i, r_d, dd - cm * r_d)
-            r_p = p[i:i + 1, :] * jnp.concatenate([inv] * 3, axis=1)
-            p = jnp.where(subN == i, r_p, p - jnp.concatenate([cm] * 3, axis=1) * r_p)
-        dinv = jnp.concatenate([dd, jnp.zeros((B, n - LANES), F32)], axis=1)
-        dinv = pltpu.roll(dinv, lax.rem(B * k - B + n, n), 1)
-        dinv = jnp.concatenate([dinv, jnp.zeros((B, LANES), F32)], axis=1)
-        inside = (laneN >= B * k) & (laneN < B * k + B)
-        ident = jnp.where(laneN == B * k + subN, 1.0, 0.0)
-        return jnp.where(inside, ident - dinv, p), jnp.where(inside, -dinv, p)
-
-    def stack(p, x):
-        ph, pm, pl_ = split3(p)
-        xh, xm, xl = split3(x)
-        join = lambda *parts: jnp.concatenate([q.astype(F32) for q in parts], axis=0).astype(BF)
-        return join(ph, ph, pm, ph, pl_, pm), join(xh, xm, xh, xl, xh, xm)
-
-    def body(k, carry):
-        p, p_old, x_old, xs_old = carry
-        ps, xs = stack(p_old[:, 0:n], x_old)
-        W[...] = W[...] - lax.dot_general(ps, xs, (((0,), (0,)), ((), ())), preferred_element_type=F32)
-        kp = pl.multiple_of(jnp.maximum(k - 1, 0) * B, B)
-        W[pl.ds(kp, B), :] = jnp.where(k > 0, xs_old, W[pl.ds(kp, B), :])
-        x_new, xs_new = chain(k, p)
-        kn = pl.multiple_of(jnp.minimum(k + 1, n // B - 1) * B, B)
-        nxt = W[pl.ds(kn, B), :]
-        col = pltpu.roll(nxt[:, 0:n], n - B * k, 1)
-        for i in range(B):
-            nxt = nxt - col[:, i:i + 1] * x_new[i:i + 1, :]
-        return nxt, p, x_new, xs_new
-
-    zero = jnp.zeros((B, n + LANES), F32)
-    _, p_old, x_old, xs_old = lax.fori_loop(0, n // B, body, (W[0:B, :], zero, zero, zero))
-    ps, xs = stack(p_old[:, 0:n], x_old)
-    w_ref[...] = W[:, n:] - lax.dot_general(ps, xs[:, n:], (((0,), (0,)), ((), ())), preferred_element_type=F32)
-    w_ref[n - B:, :] = xs_old[:, n:]
+    out, last = sweep(W, n, B)
+    w_ref[...] = out
+    w_ref[n - B:, :] = last
 
 
 def solve_call(damping, tiles):

time: 105 us -> 87.5 us (0.83)
  Pallas kernels: 95.9 us -> 78.4 us
    pallas_call x1, Pallas kernels: 27.4 us -> 9.9 us  [solve_call(): pl.pallas_call(solve_kernel, out_shape=jax.ShapeDtypeStruct((SLOTS, LANES...]
where the time goes in v2:
time: 87.5 us; the launch traced here: 86 us
  Pallas kernels  78.4 us (90%)
  local copies, waits for them, and re-layouts  5.09 us (6%)
  matrix products  1.05 us (1%)
    pallas_call x1, Pallas kernels, gram_call(): pl.pallas_call(gram_kernel, out_shape=(jax.ShapeDtypeStruct((8, 7, 8, LAN...  63.5 us
    pallas_call x1, Pallas kernels, solve_call(): pl.pallas_call(solve_kernel, out_shape=jax.ShapeDtypeStruct((SLOTS, LANES...  9.9 us
    pallas_call x1, Pallas kernels, update_call(): pl.pallas_call(update_kernel, out_shape=jax.ShapeDtypeStruct((8, 8, LANES...  5.07 us
    unnamed x10, local copies, waits for them, and re-layouts  3.31 us

profile of v2, /device:TPU:1, one launch (start us, length us, event | category | flops | bytes accessed | tf_op | source)
XLA Modules:
  0.0 86.0 jit_solution(14966476219852807324)
XLA Ops:
  0.0 0.0 copy-start
  0.0 0.7 convert_element_type.18
  0.7 0.1 convert_element_type.19
  0.8 0.0 copy-done
  0.8 1.1 %fusion = bf16[2,36,768]{2,1,0:T(8,128)(2,1)S(1)} fusion(bf16[2,36,4]{2,1,0:T(8,128)(2,1)S(1)} %convert_element_type.19, bf16[2,36,768]{2,0,1:T(2,128)(2,1)} %param.8, bf16[4,768]{1,0:T(4,128)(2,1)S(1)} %copy-done), kind=kOutput, calls=%fused_computation.1 | convolution fusion | flops 608256 | bytes 227904 | tf_op jit(solution)/shard_map/stk,kd->std/dot_general | solution.py:410
  1.9 0.2 copy.18
  2.1 0.9 %copy.14 = bf16[2,36,768]{2,1,0:T(8,128)(2,1)S(1)} copy(bf16[2,36,768]{2,0,1:T(2,128)(2,1)} %param.9) | data formatting | bytes 221184 | tf_op args[2]
  3.1 0.2 reshape.27
  3.3 0.7 pad.14.slot_ref
  4.0 0.0 copy-start.3
  4.0 0.7 copy-done.3
  4.6 63.5 %gram.1 = (f32[8,7,8,128]{3,2,1,0:T(8,128)S(1)}, bf16[48,256,128]{2,1,0:T(8,128)(2,1)S(1)}) custom-call(f32[1,2]{1,0:T(1,128)S(1)} %bitcast.15, bf16[16,48,128]{2,1,0:T(8,128)(2,1)S(1)} %bitcast.14, bf16[8,72,128]{2,1,0:T(8,128)(2,1)S(1)} %pad_bitcast_fusion.cin_ref, s32[8,128]{1,0:T(8,128)S(1)} %pad.14.slot_ref), custom_call_target="tpu_custom_call" | custom-call | tf_op jit(solution)/shard_map/gram/pallas_call | solution.py:220
  68.1 0.0 copy-start.2
  68.1 0.7 copy-done.2
  69.4 9.9 %solve.1.w_ref = f32[256,128]{1,0:T(8,128)} custom-call(f32[1,1]{1,0:T(1,128)} %bitcast.13.damp_ref, f32[8,7,8,128]{3,2,1,0:T(8,128)} %copy-done.2), custom_call_target="tpu_custom_call" | custom-call | tf_op jit(solution)/shard_map/solve/pallas_call | solution.py:349
  79.3 0.0 copy-start.1
  79.3 0.9 %copy-done.1 = f32[256,128]{1,0:T(8,128)S(1)} copy-done((f32[256,128]{1,0:T(8,128)S(1)}, f32[256,128]{1,0:T(8,128)}, u32[]{:S(2)}) %copy-start.1) | copy-done | bytes 131096
  80.2 5.1 %update.1 = f32[8,8,128]{2,1,0:T(8,128)S(1)} custom-call(f32[256,128]{1,0:T(8,128)S(1)} %copy-done.1, bf16[48,256,128]{2,1,0:T(8,128)(2,1)S(1)} %get-tuple-element.8.cen_ref), custom_call_target="tpu_custom_call" | custom-call | tf_op jit(solution)/shard_map/update/pallas_call | solution.py:396
  85.3 0.7 reshape.29
  (6 shorter events, 0.1 us)
Async XLA Ops:
  0.0 0.8 copy-start
  4.0 0.7 copy-start.3
  68.1 0.7 copy-start.2
  79.3 0.9 %copy-start.1 = (f32[256,128]{1,0:T(8,128)S(1)}, f32[256,128]{1,0:T(8,128)}, u32[]{:S(2)}) copy-start(f32[256,128]{1,0:T(8,128)} %solve.1.w_ref) | copy-start | bytes 393220

commit v3 on v2

--- a/solution.py
+++ b/solution.py
@@ -43,15 +43,27 @@
     )
 
 
-def gram_kernel(energy_ref, lin_ref, cin_ref, slot_ref, out_ref, cen_ref,
-                lall, call, rbuf, gacc, gp, rr, ssum, cr, tile, s2,
+def rel(r):
+    m = r // 2
+    return r % 2, m + (m // 2) * (1 - 2 * (m % 2))
+
+
+def gram_kernel(lin_ref, cin_ref, slot_ref, out_ref, erow_ref, cen_ref,
+                lraw, lpk, call, rbuf, esc, gacc, gp, cbuf, rr, s1, cr, s2,
                 l1s, l1r, c1s, c1r, c2s, c2r, c3s, c3r, l2s, l2r,
-                rs_s, rs_r, cs_s, cs_r, bc_s, bc_r, ag_s, ag_r):
+                a_s, a_r, b_s, b_r, x_s, x_r, d_s, d_r, e_s, e_r):
     g, d, x_hi, core, z, rb = place()
     a = g * 4 + z
     b = flip(rb, x_hi)
-    chip = x_hi * 4 + z
+    q, y = b % 2, b // 2
     partner = (x_hi * 2 + 1 - core, d)
+
+    def cpos(du, dv, other=0):
+        c = core + other * (1 - 2 * core)
+        return (((x_hi + du) % 2) * 2 + c) * 4 + (z + dv) % 4
+
+    def lpos(du, dv):
+        return ((y + dv) % 4) * 2 + (q + du) % 2
 
     barrier = pltpu.get_barrier_semaphore()
     for k in range(1, 16):
@@ -65,62 +77,148 @@
     def start(copy):
         copy.start()
         sends.append(copy)
+
+    def arrived(ref, sem):
+        remote(ref, ref, sem, sem, partner).wait_recv()
 
     for k in range(1, 8):
         bt = (b + k) % 8
         start(remote(cin_ref.at[bt], call.at[a, b], c1s.at[k], c1r.at[b], column_device(a, bt)))
     for k in range(1, 16):
         at = (a + k) % 16
-        start(remote(lin_ref.at[at], lall.at[b, a], l1s.at[k], l1r.at[a], column_device(at, b)))
+        start(remote(lin_ref.at[at], lraw.at[a], l1s.at[k], l1r.at[a], column_device(at, b)))
     call[a, b] = cin_ref[b]
-    lall[b, a] = lin_ref[a]
+    lraw[a] = lin_ref[a]
+
+    def chalf(p, h):
+        return call.at[p] if h is None else call.at[p, pl.ds(4 * h, 4)]
+
+    def lhalf(p, h):
+        return lpk.at[p] if h is None else lpk.at[p, pl.ds(5 * h, 5 - h)]
+
+    slot_c, slot_l = [0], [0]
+
+    def csend(org, h, to, seen):
+        ref = chalf(cpos(*org), h)
+        start(remote(ref, ref, c2s.at[slot_c[0]], c2r.at[seen[0] * 4 + seen[1], h or 0], column_device(cpos(*to), b)))
+        slot_c[0] += 1
+
+    def lsend(org, h, to, seen):
+        ref = lhalf(lpos(*org), h)
+        start(remote(ref, ref, l2s.at[slot_l[0]], l2r.at[seen[0] * 4 + seen[1], h or 0], column_device(a, lpos(*to))))
+        slot_l[0] += 1
+
+    def over(org, h=None):
+        ref = chalf(cpos(*org), h)
+        n = org[0] * 4 + org[1]
+        start(remote(ref, ref, c3s.at[n, h or 0], c3r.at[n, h or 0], partner))
+
+    def cwait(org, h=None):
+        arrived(chalf(cpos(*org), h), c2r.at[org[0] * 4 + org[1], h or 0])
+
+    def owait(org, h=None):
+        arrived(chalf(cpos(*org, 1), h), c3r.at[org[0] * 4 + org[1], h or 0])
+
+    def lwait(org, h=None):
+        arrived(lhalf(lpos(*org), h), l2r.at[org[0] * 4 + org[1], h or 0])
+
+    HERE, PAIR, UP, DOWN = (0, 0), (1, 0), (0, 1), (0, 3)
 
     for k in range(1, 8):
         bs = (b + 8 - k) % 8
-        remote(call.at[a, bs], call.at[a, bs], c1s.at[k], c1r.at[bs], partner).wait_recv()
-    for k in range(1, 8):
-        ct = (chip + k) % 8
-        at = (ct // 4) * 8 + core * 4 + ct % 4
-        start(remote(call.at[a], call.at[a], c2s.at[k], c2r.at[chip], column_device(at, b)))
-    start(remote(call.at[a], call.at[a], c3s.at[0], c3r.at[chip], partner))
+        arrived(call.at[a, bs], c1r.at[bs])
+    csend(HERE, None, PAIR, (1, 0))
+    csend(HERE, None, UP, (0, 3))
+    csend(HERE, None, DOWN, (0, 1))
+    over(HERE)
 
     for k in range(1, 16):
         asrc = (a + 16 - k) % 16
-        remote(lall.at[b, asrc], lall.at[b, asrc], l1s.at[k], l1r.at[asrc], partner).wait_recv()
-    for k in range(1, 8):
-        bt = (b + k) % 8
-        start(remote(lall.at[b], lall.at[b], l2s.at[k], l2r.at[b], column_device(a, bt)))
-
-    for k in range(1, 8):
-        cs = (chip + 8 - k) % 8
-        asrc = (cs // 4) * 8 + core * 4 + cs % 4
-        remote(call.at[asrc], call.at[asrc], c2s.at[k], c2r.at[cs], partner).wait_recv()
-        start(remote(call.at[asrc], call.at[asrc], c3s.at[k], c3r.at[cs], partner))
-    for k in range(0, 8):
-        cs = (chip + 8 - k) % 8
-        asrc = (cs // 4) * 8 + (1 - core) * 4 + cs % 4
-        remote(call.at[asrc], call.at[asrc], c3s.at[k], c3r.at[cs], partner).wait_recv()
-    for k in range(1, 8):
-        bs = (b + 8 - k) % 8
-        remote(lall.at[bs], lall.at[bs], l2s.at[k], l2r.at[bs], partner).wait_recv()
+        arrived(lraw.at[asrc], l1r.at[asrc])
+    packed = jnp.concatenate([lraw[s][:, :ROWS2] for s in range(16)], axis=1)
+    for t in range(9):
+        lpk[b, t] = packed[:, t * LANES:(t + 1) * LANES]
+    lsend(HERE, None, PAIR, (1, 0))
+    lsend(HERE, None, UP, (0, 3))
+    lsend(HERE, None, DOWN, (0, 1))
+
+    cwait(PAIR)
+    csend(PAIR, None, UP, (1, 3))
+    csend(PAIR, None, DOWN, (1, 1))
+    over(PAIR)
+    lwait(PAIR)
+    lsend(PAIR, None, UP, (1, 3))
+    lsend(PAIR, None, DOWN, (1, 1))
+    for u in range(2):
+        cwait((u, 3))
+        csend((u, 3), 0, UP, (u, 2))
+        over((u, 3))
+        cwait((u, 1))
+        csend((u, 1), 1, DOWN, (u, 2))
+        over((u, 1))
+        lwait((u, 3))
+        lsend((u, 3), 0, UP, (u, 2))
+        lwait((u, 1))
+        lsend((u, 1), 1, DOWN, (u, 2))
 
     lane = lax.broadcasted_iota(jnp.int32, (IB, LANES), 1)
-    first = jnp.where(lane < TOKS, 1.0, 0.0).astype(BF)
-    second = jnp.where((lane >= TOKS) & (lane < ROWS2), 1.0, 0.0).astype(BF)
-
-    def rows_step(asrc, carry):
-        high = asrc // 8
-        for bs in range(8):
-            left = lall[bs, asrc]
-            left = jnp.concatenate([left * first, left * second], axis=0)
-            prod = lax.dot_general(left[:, :ROWS2], call[asrc, bs], (((1,), (0,)), ((), ())),
-                                   preferred_element_type=F32)
-            at = asrc * 8 + flip(bs, high)
-            rbuf[pl.ds(pl.multiple_of(at * 2 * IB, 2 * IB), 2 * IB), :] = (
-                prod * (1.0 / math.sqrt(TOKS))).astype(BF).astype(F32)
-        return carry
-
-    lax.fori_loop(0, 16, rows_step, 0)
+    first = jnp.where(lane < TOKS, 1.0, 0.0)
+    second = jnp.where((lane >= TOKS) & (lane < ROWS2), 1.0, 0.0)
+    lane1 = lax.broadcasted_iota(jnp.int32, (1, LANES), 1)
+    scale = jnp.where(lane1 < JB, 1.0 / math.sqrt(TOKS), 0.0)
+
+    def rows_of(other, rc, lsteps):
+        asrc = cpos(*rel(rc), other)
+        off = asrc * ROWS2
+        t0 = off // LANES
+        o = off % LANES
+        t1 = jnp.minimum(t0 + 1, 8)
+        shift = (LANES - o) % LANES
+        for rl in lsteps:
+            bs = lpos(*rel(rl))
+            lo = pltpu.roll(lpk[bs, t0].astype(F32), shift, 1)
+            hi = pltpu.roll(lpk[bs, t1].astype(F32), shift, 1)
+            left = jnp.where(lane < LANES - o, lo, hi)
+            left = jnp.concatenate([left * first, left * second], axis=0).astype(BF)
+            right = call[asrc, bs]
+            prod = lax.dot_general(left[:, :ROWS2], right, (((1,), (0,)), ((), ())), preferred_element_type=F32)
+            at = asrc * 8 + flip(bs, asrc // 8)
+            rbuf[pl.ds(pl.multiple_of(at * 2 * IB, 2 * IB), 2 * IB), :] = (prod * scale).astype(BF).astype(F32)
+            esc[pl.ds(at, 1), :] = right.astype(F32)[0:1, :]
+
+    def rows_loop(other, lo, hi, lsteps):
+        def body(rc, carry):
+            rows_of(other, rc, lsteps)
+            return carry
+        lax.fori_loop(lo, hi, body, 0)
+
+    rows_loop(0, 0, 6, range(6))
+    for org in (HERE, PAIR, DOWN, UP, (1, 3), (1, 1)):
+        owait(org)
+    rows_loop(1, 0, 6, range(6))
+    for u in range(2):
+        for h in range(2):
+            cwait((u, 2), h)
+            over((u, 2), h)
+        for h in range(2):
+            lwait((u, 2), h)
+    for other in range(2):
+        rows_loop(other, 0, 6, range(6, 8))
+    rows_loop(0, 6, 8, range(8))
+    for u in range(2):
+        for h in range(2):
+            owait((u, 2), h)
+    rows_loop(1, 6, 8, range(8))
+
+    parts = esc[...]
+    pos = lax.broadcasted_iota(jnp.int32, (LANES, LANES), 0) * 2
+    for half in range(2):
+        row = jnp.zeros((1, LANES), F32)
+        for k in range(2):
+            e = parts[:, JB + 3 * k:JB + 3 * k + 1] + parts[:, JB + 3 * k + 1:JB + 3 * k + 2] + parts[:, JB + 3 * k + 2:JB + 3 * k + 3]
+            hit = slot_ref[half:half + 1, :] == pos + k
+            row = row + jnp.sum(jnp.where(hit, e, 0.0), axis=0, keepdims=True)
+        erow_ref[half:half + 1, :] = row
 
     gacc[...] = jnp.zeros_like(gacc)
     inv_root = 1.0 / math.sqrt(WIDTH * WIDTH)
@@ -144,106 +242,84 @@
         blk, w = t // 16, t % 16
         r0 = (0, 128, 128)[blk] + 8 * w
         c0 = (0, 0, 128)[blk]
-        gp[t // 6, t % 6] = gacc[r0:r0 + 8, c0:c0 + 128]
-    slots = slot_ref[...]
-    base = (g * 32 + d) * 2
-    mine = jnp.where(slots == base, energy_ref[0, 0], 0.0) + jnp.where(slots == base + 1, energy_ref[0, 1], 0.0)
-    for r in range(8):
-        gp[r, 6] = mine if r == 0 else jnp.zeros_like(mine)
-
+        gp[t // 24, (t % 24) // 3, t % 3] = gacc[r0:r0 + 8, c0:c0 + 128]
+
+    start(remote(gp.at[1 - core], cbuf, a_s, a_r, partner))
+    arrived(cbuf, a_r)
+    cbuf[...] = cbuf[...] + gp[core]
     for k in range(1, 8):
         bt = (b + k) % 8
-        start(remote(gp.at[bt], rr.at[b], rs_s.at[k], rs_r.at[b], column_device(a, bt)))
+        start(remote(cbuf.at[bt], rr.at[b], b_s.at[k], b_r.at[b], column_device(a, bt)))
+    rr[b] = cbuf[b]
     for k in range(1, 8):
         bs = (b + 8 - k) % 8
-        remote(rr.at[bs], rr.at[bs], rs_s.at[k], rs_r.at[bs], partner).wait_recv()
-    rr[b] = gp[b]
+        arrived(rr.at[bs], b_r.at[bs])
     total = rr[0]
     for k in range(1, 8):
         total = total + rr[k]
-    ssum[...] = total
-
-    for j in range(7):
-        owner = (j % 2) * 8 + j // 2
-
-        @pl.when(a != owner)
-        def _():
-            remote(ssum.at[j], cr.at[a], cs_s.at[j], cs_r.at[a], column_device(owner + 0 * a, b)).start()
-
-    for j in range(7):
-        owner = (j % 2) * 8 + j // 2
-
-        @pl.when(a == owner)
-        def _():
-            for k in range(1, 16):
-                asrc = (a + k) % 16
-                remote(cr.at[asrc], cr.at[asrc], cs_s.at[j], cs_r.at[asrc], partner).wait_recv()
-            cr[owner] = ssum[j]
-            t = cr[0]
-            for k in range(1, 16):
-                t = t + cr[k]
-            s2[j] = t
-            for k in range(1, 16):
-                at = (a + k) % 16
-                remote(s2.at[j], s2.at[j], bc_s.at[k], bc_r.at[j], column_device(at, b)).start()
-
-    for j in range(7):
-        owner = (j % 2) * 8 + j // 2
-
-        @pl.when(a != owner)
-        def _():
-            remote(ssum.at[j], cr.at[a], cs_s.at[j], cs_r.at[a], partner).wait_send()
-            remote(s2.at[j], s2.at[j], bc_s.at[0], bc_r.at[j], partner).wait_recv()
-
+    s1[...] = total
+    chip = x_hi * 4 + z
+    cr[chip] = total
+    for k in range(1, 8):
+        ct = (chip + k) % 8
+        start(remote(s1, cr.at[chip], x_s.at[k], x_r.at[chip], column_device((ct // 4) * 8 + core * 4 + ct % 4, b)))
+    for k in range(1, 8):
+        cs = (chip + 8 - k) % 8
+        arrived(cr.at[cs], x_r.at[cs])
+    total = cr[0]
+    for k in range(1, 8):
+        total = total + cr[k]
+    s2[...] = total
+    out_ref[core, b] = total
     for k in range(1, 8):
         bt = (b + k) % 8
-        start(remote(s2, out_ref.at[b], ag_s.at[k], ag_r.at[b], column_device(a, bt)))
-    out_ref[b] = s2[...]
+        start(remote(s2, out_ref.at[core, b], d_s.at[k], d_r.at[b], column_device(a, bt)))
+    start(remote(s2, out_ref.at[core, b], e_s.at[0], e_r.at[b], partner))
     for k in range(1, 8):
         bs = (b + 8 - k) % 8
-        remote(out_ref.at[bs], out_ref.at[bs], ag_s.at[k], ag_r.at[bs], partner).wait_recv()
+        arrived(out_ref.at[core, bs], d_r.at[bs])
+        start(remote(out_ref.at[core, bs], out_ref.at[core, bs], e_s.at[k], e_r.at[bs], partner))
+    for k in range(8):
+        bs = (b + 8 - k) % 8
+        arrived(out_ref.at[1 - core, bs], e_r.at[bs])
 
     for copy in sends:
         copy.wait_send()
-    for j in range(7):
-        owner = (j % 2) * 8 + j // 2
-
-        @pl.when(a == owner)
-        def _():
-            for k in range(1, 16):
-                remote(s2.at[j], s2.at[j], bc_s.at[k], bc_r.at[j], partner).wait_send()
-
-
-def gram_call(energy, lin, cin, slots):
+
+
+def gram_call(lin, cin, slots):
     dma = pltpu.SemaphoreType.DMA
     vmem = pl.BlockSpec(memory_space=pltpu.VMEM)
     return pl.pallas_call(
         gram_kernel,
         out_shape=(
-            jax.ShapeDtypeStruct((8, 7, 8, LANES), F32),
+            jax.ShapeDtypeStruct((2, 8, 3, 8, LANES), F32),
+            jax.ShapeDtypeStruct((2, LANES), F32),
             jax.ShapeDtypeStruct((IB, SLOTS, LANES), BF),
         ),
-        in_specs=[pl.BlockSpec(memory_space=pltpu.SMEM), vmem, vmem, vmem],
-        out_specs=(vmem, vmem),
+        in_specs=[vmem, vmem, vmem],
+        out_specs=(vmem, vmem, vmem),
         scratch_shapes=[
-            pltpu.VMEM((8, 16, IB, LANES), BF),
+            pltpu.VMEM((16, IB, LANES), BF),
+            pltpu.VMEM((8, 9, IB, LANES), BF),
             pltpu.VMEM((16, 8, ROWS2, LANES), BF),
             pltpu.VMEM((SLOTS * IB, LANES), F32),
+            pltpu.VMEM((LANES, LANES), F32),
             pltpu.VMEM((SLOTS, SLOTS), F32),
-            pltpu.VMEM((8, 7, 8, LANES), F32),
-            pltpu.VMEM((8, 7, 8, LANES), F32),
-            pltpu.VMEM((7, 8, LANES), F32),
-            pltpu.VMEM((16, 8, LANES), F32),
-            pltpu.VMEM((8, LANES), F32),
-            pltpu.VMEM((7, 8, LANES), F32),
-            dma((16,)), dma((16,)), dma((8,)), dma((8,)), dma((8,)), dma((8,)),
-            dma((8,)), dma((8,)), dma((8,)), dma((8,)),
-            dma((8,)), dma((8,)), dma((8,)), dma((16,)), dma((16,)), dma((8,)), dma((8,)), dma((8,)),
+            pltpu.VMEM((2, 8, 3, 8, LANES), F32),
+            pltpu.VMEM((8, 3, 8, LANES), F32),
+            pltpu.VMEM((8, 3, 8, LANES), F32),
+            pltpu.VMEM((3, 8, LANES), F32),
+            pltpu.VMEM((8, 3, 8, LANES), F32),
+            pltpu.VMEM((3, 8, LANES), F32),
+            dma((16,)), dma((16,)), dma((8,)), dma((8,)), dma((9,)), dma((8, 2)),
+            dma((8, 2)), dma((8, 2)), dma((9,)), dma((8, 2)),
+            dma(()), dma(()), dma((8,)), dma((8,)), dma((8,)), dma((8,)), dma((8,)), dma((8,)), dma((8,)), dma((8,)),
         ],
         compiler_params=pltpu.CompilerParams(
             collective_id=0, has_side_effects=True, vmem_limit_bytes=48 * 1024 * 1024),
         name="gram",
-    )(energy, lin, cin, slots)
+    )(lin, cin, slots)
 
 
 def split3(x):
@@ -323,16 +399,15 @@
     return W[:, n:] - lax.dot_general(ps, xs, tn, preferred_element_type=F32), xso[T]
 
 
-def solve_kernel(damp_ref, gt_ref, w_ref, W):
+def solve_kernel(damp_ref, gt_ref, erow_ref, w_ref, W):
     n, B = SLOTS, 8
     for t in range(48):
         blk, w = t // 16, t % 16
         r0 = (0, 128, 128)[blk] + 8 * w
         c0 = (0, 0, 128)[blk]
-        W[r0:r0 + 8, c0:c0 + 128] = gt_ref[t // 6, t % 6]
+        W[r0:r0 + 8, c0:c0 + 128] = gt_ref[t // 24, (t % 24) // 3, t % 3]
     W[0:128, 128:256] = W[128:256, 0:128].T
-    energy = gt_ref[0, 6]
-    e_row = jnp.concatenate([energy[0:1, :], energy[1:2, :]], axis=1)
+    e_row = jnp.concatenate([erow_ref[0:1, :], erow_ref[1:2, :]], axis=1)
     sh = e_row - jnp.sum(e_row, axis=1, keepdims=True) * (1.0 / n)
     rows = lax.broadcasted_iota(jnp.int32, (n, n), 0)
     cols = lax.broadcasted_iota(jnp.int32, (n, n), 1)
@@ -344,16 +419,16 @@
     w_ref[n - B:, :] = last
 
 
-def solve_call(damping, tiles):
+def solve_call(damping, tiles, erow):
     vmem = pl.BlockSpec(memory_space=pltpu.VMEM)
     return pl.pallas_call(
         solve_kernel,
         out_shape=jax.ShapeDtypeStruct((SLOTS, LANES), F32),
-        in_specs=[pl.BlockSpec(memory_space=pltpu.SMEM), vmem],
+        in_specs=[pl.BlockSpec(memory_space=pltpu.SMEM), vmem, vmem],
         out_specs=vmem,
         scratch_shapes=[pltpu.VMEM((SLOTS, SLOTS + LANES), F32)],
         name="solve",
-    )(damping, tiles)
+    )(damping, tiles, erow)
 
 
 def update_kernel(w_ref, cen_ref, out_ref, u, send, recv):
@@ -411,9 +486,13 @@
     layer_in = (layer_acts.astype(F32) + embedded).astype(BF)
     lin = jnp.pad(layer_in.reshape(ROWS2, WIDTH).T, ((0, 0), (0, LANES - ROWS2))).reshape(16, IB, LANES)
     cin = jnp.pad(cotangent.reshape(ROWS2, 8, JB), ((0, 0), (0, 0), (0, LANES - JB))).transpose(1, 0, 2)
-    slots = jnp.pad(slot_sample.reshape(2, LANES), ((0, 6), (0, 0)), constant_values=-1)
-    tiles, cen = gram_call(energies.reshape(1, 2), lin, cin, slots)
-    weights = solve_call(damping.reshape(1, 1), tiles)
+    high = lax.reduce_precision(energies, 8, 7)
+    mid = lax.reduce_precision(energies - high, 8, 7)
+    parts = jnp.stack([high, mid, energies - high - mid], axis=1).reshape(1, 1, 6).astype(BF)
+    parts = jnp.pad(parts, ((0, 0), (0, ROWS2 - 1), (JB, LANES - JB - 6)))
+    cin = cin + parts
+    tiles, erow, cen = gram_call(lin, cin, slot_sample.reshape(2, LANES))
+    weights = solve_call(damping.reshape(1, 1), tiles, erow)
     pieces = update_call(weights, cen)
     return pieces[:, :6, :JB].transpose(1, 0, 2).reshape(-1)
 

time: 87.5 us -> 77.9 us (0.89); the launches traced: 86 us -> 77.6 us
  Pallas kernels: 78.4 us -> 69.2 us
    pallas_call x1, Pallas kernels: 63.5 us -> 54.2 us  [gram_call(): pl.pallas_call(gram_kernel, out_shape=(jax.ShapeDtypeStruct((2, 8, 3, 8,...]
    unnamed x10 -> x12, local copies, waits for them, and re-layouts: 3.31 us -> 3.88 us
where the time goes in v3:
time: 77.9 us; the launch traced here: 77.6 us
  Pallas kernels  69.2 us (89%)
  local copies, waits for them, and re-layouts  5.21 us (7%)
  other arithmetic  1.42 us (2%)
  matrix products  1.05 us (1%)
    pallas_call x1, Pallas kernels, gram_call(): pl.pallas_call(gram_kernel, out_shape=(jax.ShapeDtypeStruct((2, 8, 3, 8,...  54.2 us
    pallas_call x1, Pallas kernels, solve_call(): pl.pallas_call(solve_kernel, out_shape=jax.ShapeDtypeStruct((SLOTS, LANES...  9.88 us
    pallas_call x1, Pallas kernels, update_call(): pl.pallas_call(update_kernel, out_shape=jax.ShapeDtypeStruct((8, 8, LANES...  5.07 us
    unnamed x12, local copies, waits for them, and re-layouts  3.88 us

profile of v3, /device:TPU:1, one launch (start us, length us, event | category | flops | bytes accessed | tf_op | source)
XLA Modules:
  0.0 77.6 jit_solution(2187010945855478145)
XLA Ops:
  0.0 0.0 copy-start
  0.0 0.7 fusion.2
  0.7 0.1 copy.17
  0.8 0.1 convert_element_type.35
  0.9 0.1 pad_bitcast_fusion
  1.0 0.9 %copy.15 = bf16[2,36,768]{2,1,0:T(8,128)(2,1)S(1)} copy(bf16[2,36,768]{2,0,1:T(2,128)(2,1)} %param.9) | data formatting | bytes 221184 | tf_op args[2]
  1.9 0.2 reshape.37
  2.1 0.7 convert_element_type.32
  2.8 0.1 convert_element_type.33
  2.9 0.0 copy-done
  2.9 1.1 %fusion = bf16[2,36,768]{2,1,0:T(8,128)(2,1)S(1)} fusion(bf16[2,36,4]{2,1,0:T(8,128)(2,1)S(1)} %convert_element_type.33, bf16[2,36,768]{2,0,1:T(2,128)(2,1)} %param.8, bf16[4,768]{1,0:T(4,128)(2,1)S(1)} %copy-done), kind=kOutput, calls=%fused_computation.1 | convolution fusion | flops 608256 | bytes 227904 | tf_op jit(solution)/shard_map/stk,kd->std/dot_general | solution.py:485
  4.0 0.2 copy.20
  4.3 0.0 copy-start.3
  4.3 0.7 copy-done.3
  4.9 54.2 %gram.1 = (f32[2,8,3,8,128]{4,3,2,1,0:T(8,128)S(1)}, f32[2,128]{1,0:T(2,128)S(1)}, bf16[48,256,128]{2,1,0:T(8,128)(2,1)S(1)}) custom-call(bf16[16,48,128]{2,1,0:T(8,128)(2,1)S(1)} %bitcast.21, bf16[8,72,128]{2,1,0:T(8,128)(2,1)S(1)} %add_bitcast_fusion.cin_ref, s32[2,128]{1,0:T(2,128)S(1)} %bitcast.22), custom_call_target="tpu_custom_call" | custom-call | tf_op jit(solution)/shard_map/gram/pallas_call | solution.py:293
  59.2 0.0 copy-start.2
  59.2 0.7 copy-done.2
  59.8 0.0 copy-start.4
  59.8 0.6 copy-done.4
  61.1 9.9 %solve.1.w_ref = f32[256,128]{1,0:T(8,128)} custom-call(f32[1,1]{1,0:T(1,128)} %bitcast.20.damp_ref, f32[2,8,3,8,128]{4,3,2,1,0:T(8,128)} %copy-done.2, f32[2,128]{1,0:T(2,128)} %copy-done.4), custom_call_target="tpu_custom_call" | custom-call | tf_op jit(solution)/shard_map/solve/pallas_call | solution.py:424
  70.9 0.0 copy-start.1
  70.9 0.9 %copy-done.1 = f32[256,128]{1,0:T(8,128)S(1)} copy-done((f32[256,128]{1,0:T(8,128)S(1)}, f32[256,128]{1,0:T(8,128)}, u32[]{:S(2)}) %copy-start.1) | copy-done | bytes 131096
  71.8 5.1 %update.1 = f32[8,8,128]{2,1,0:T(8,128)S(1)} custom-call(f32[256,128]{1,0:T(8,128)S(1)} %copy-done.1, bf16[48,256,128]{2,1,0:T(8,128)(2,1)S(1)} %get-tuple-element.10.cen_ref), custom_call_target="tpu_custom_call" | custom-call | tf_op jit(solution)/shard_map/update/pallas_call | solution.py:471
  76.9 0.7 reshape.39
  (7 shorter events, 0.2 us)
Async XLA Ops:
  0.0 2.9 %copy-start = (bf16[4,768]{1,0:T(4,128)(2,1)S(1)}, bf16[4,768]{1,0:T(4,128)(2,1)}, u32[]{:S(2)}) copy-start(bf16[4,768]{1,0:T(4,128)(2,1)} %param.10) | copy-start | bytes 18436
  4.3 0.7 copy-start.3
  59.2 0.7 copy-start.2
  59.8 0.6 copy-start.4
  70.9 0.9 %copy-start.1 = (f32[256,128]{1,0:T(8,128)S(1)}, f32[256,128]{1,0:T(8,128)}, u32[]{:S(2)}) copy-start(f32[256,128]{1,0:T(8,128)} %solve.1.w_ref) | copy-start | bytes 393220

commit v4 on v3

v4 whole, which is shorter than its diff:
```python
import math

import jax
import jax.numpy as jnp
from jax import lax
from jax.experimental import pallas as pl
from jax.experimental.pallas import tpu as pltpu
from jax.sharding import PartitionSpec as P

F32 = jnp.float32
BF = jnp.bfloat16
MESH = pl.DeviceIdType.MESH
SLOTS = 256
WIDTH = 768
SITES = 144
PATCH = 4
TOKS = 36
IB = 48
JB = 96
ROWS2 = 2 * TOKS
LANES = 128


def flip(index, high):
    return index + high * (1 - 2 * (index % 2))


def place():
    g = lax.axis_index("grp")
    d = lax.axis_index("dev")
    x_hi, core = g // 2, g % 2
    z, rb = d // 8, d % 8
    return g, d, x_hi, core, z, rb


def column_device(a, b):
    g, z = a // 4, a % 4
    return (g, z * 8 + flip(b, g // 2))


def remote(src, dst, send_sem, recv_sem, device):
    return pltpu.make_async_remote_copy(
        src_ref=src, dst_ref=dst, send_sem=send_sem, recv_sem=recv_sem,
        device_id=device, device_id_type=MESH,
    )


def rel(r):
    m = r // 2
    return r % 2, m + (m // 2) * (1 - 2 * (m % 2))


def split3(x):
    high = x.astype(BF)
    rest = x - high.astype(F32)
    mid = rest.astype(BF)
    return high, mid, (rest - mid.astype(F32)).astype(BF)


def recip(x):
    r = pl.reciprocal(x, approx=True)
    return r * (2.0 - x * r)


def sweep(W, n, B):
    sub = lax.broadcasted_iota(jnp.int32, (B, LANES), 0)
    lane = lax.broadcasted_iota(jnp.int32, (B, LANES), 1)
    masks = [sub == i for i in range(B)]
    T = n // LANES

    def chain(k, p):
        t0, l0 = (B * k) // LANES, (B * k) % LANES
        c = [jnp.broadcast_to(p[t0][:, l0 + j:l0 + j + 1], (B, LANES)) for j in range(B)]
        p = list(p)
        for i in range(B):
            inv = recip(c[i][i:i + 1, :])
            ci = c[i]
            for j in range(B):
                if j == i:
                    c[j] = jnp.where(masks[i], inv, -ci * inv)
                else:
                    t = c[j][i:i + 1, :] * inv
                    c[j] = jnp.where(masks[i], t, c[j] - ci * t)
            for v in range(T + 1):
                r = p[v][i:i + 1, :] * inv
                p[v] = jnp.where(masks[i], r, p[v] - ci * r)
        dinv = jnp.zeros((B, LANES), F32)
        for j in range(B):
            dinv = jnp.where(lane == l0 + j, c[j], dinv)
        inside = (lane >= l0) & (lane < l0 + B)
        ident = jnp.where(lane == l0 + sub, 1.0, 0.0)
        x, xs = list(p), list(p)
        x[t0] = jnp.where(inside, ident - dinv, p[t0])
        xs[t0] = jnp.where(inside, -dinv, p[t0])
        return x, xs

    def stack(p, x):
        ph, pm, pl_ = split3(p)
        xh, xm, xl = split3(x)
        join = lambda *parts: jnp.concatenate([q.astype(F32) for q in parts], axis=0).astype(BF)
        return join(ph, ph, pm, ph, pl_, pm), join(xh, xm, xh, xl, xh, xm)

    cat = lambda v: jnp.concatenate(v, axis=1)
    tn = (((0,), (0,)), ((), ()))
    p = [W[0:B, v * LANES:(v + 1) * LANES] for v in range(T + 1)]
    old = None
    for k in range(n // B):
        if old is not None:
            po, xo, xso = old
            ps, xs = stack(cat(po[:T]), cat(xo))
            W[...] = W[...] - lax.dot_general(ps, xs, tn, preferred_element_type=F32)
            W[B * (k - 1):B * k, :] = cat(xso)
        x, xs = chain(k, p)
        old = (p, x, xs)
        if k + 1 < n // B:
            nxt = [W[B * (k + 1):B * (k + 2), v * LANES:(v + 1) * LANES] for v in range(T + 1)]
            t0, l0 = (B * k) // LANES, (B * k) % LANES
            cols = [nxt[t0][:, l0 + i:l0 + i + 1] for i in range(B)]
            for v in range(T + 1):
                terms = [cols[i] * x[v][i:i + 1, :] for i in range(B)]
                while len(terms) > 1:
                    terms = [terms[q] + terms[q + 1] for q in range(0, len(terms), 2)]
                nxt[v] = nxt[v] - terms[0]
            p = nxt
    po, xo, xso = old
    ps, xs = stack(cat(po[:T]), xo[T])
    return W[:, n:] - lax.dot_general(ps, xs, tn, preferred_element_type=F32), xso[T]


def prepare(spin, acts, cot, embed, energy_ref, stage, cstage, lin, cin):
    sub = lax.broadcasted_iota(jnp.int32, (40, SITES), 0)
    site = lax.broadcasted_iota(jnp.int32, (40, SITES), 1)
    spins = spin[...].astype(F32)
    patches = jnp.concatenate(
        [jnp.where(site // PATCH == sub, spins[s:s + 1, :], 0.0) for s in range(2)], axis=0).astype(BF)
    turn = lax.broadcasted_iota(jnp.int32, (SITES, WIDTH), 0) % PATCH
    table = embed[...].astype(F32)
    spread = jnp.zeros((SITES, WIDTH), F32)
    for k in range(PATCH):
        spread = jnp.where(turn == k, table[k:k + 1, :], spread)
    added = jnp.dot(patches, spread.astype(BF), preferred_element_type=F32)
    for s in range(2):
        stage[TOKS * s:TOKS * (s + 1), :] = (acts[s].astype(F32) + added[40 * s:40 * s + TOKS, :]).astype(BF).astype(F32)
    stage[ROWS2:, :] = jnp.zeros((LANES - ROWS2, WIDTH), F32)
    for v in range(WIDTH // LANES):
        lin[v * LANES:(v + 1) * LANES, :] = stage[:, v * LANES:(v + 1) * LANES].T.astype(BF)
    lane = lax.broadcasted_iota(jnp.int32, (TOKS, LANES), 1)
    row = lax.broadcasted_iota(jnp.int32, (TOKS, LANES), 0)
    high, mid, low = (t.astype(F32) for t in split3(
        jnp.where(lane < JB + 3, jnp.full((TOKS, LANES), energy_ref[0], F32), jnp.full((TOKS, LANES), energy_ref[1], F32))))
    third = lane % 3
    parts = jnp.where(third == 0, high, jnp.where(third == 1, mid, low))
    parts = jnp.where((row == 0) & (lane < JB + 6), parts, 0.0)
    for s in range(2):
        x = cot[s].astype(F32)
        for b in range(8):
            t, o = (JB * b) // LANES, (JB * b) % LANES
            piece = x[:, t * LANES:(t + 1) * LANES]
            if o:
                piece = pltpu.roll(piece, LANES - o, 1)
                if LANES - o < JB:
                    piece = jnp.where(lane < LANES - o, piece, pltpu.roll(x[:, (t + 1) * LANES:(t + 2) * LANES], LANES - o, 1))
            cstage[b, TOKS * s:TOKS * (s + 1), :] = jnp.where(lane < JB, piece, parts if s == 0 else 0.0)
    cin[...] = cstage[...].astype(BF)


def main_kernel(energy_ref, damp_ref, spin_hbm, acts_hbm, cot_hbm, embed_hbm, slot_hbm, out_ref,
                spin_v, acts_v, cot_v, embed_v, slot_ref, in_sem, stage, cstage, lin_ref, cin_ref,
                gt, erow_ref, cen_ref, W, wv, upd, ur, f_s, f_r,
                lraw, lpk, call, rbuf, esc, gacc, gp, cbuf, rr, s1, cr, s2,
                l1s, l1r, c1s, c1r, c2s, c2r, c3s, c3r, l2s, l2r,
                a_s, a_r, b_s, b_r, x_s, x_r, d_s, d_r, e_s, e_r):
    g, d, x_hi, core, z, rb = place()
    a = g * 4 + z
    b = flip(rb, x_hi)
    q, y = b % 2, b // 2
    partner = (x_hi * 2 + 1 - core, d)

    def cpos(du, dv, other=0):
        c = core + other * (1 - 2 * core)
        return (((x_hi + du) % 2) * 2 + c) * 4 + (z + dv) % 4

    def lpos(du, dv):
        return ((y + dv) % 4) * 2 + (q + du) % 2

    barrier = pltpu.get_barrier_semaphore()
    for k in range(1, 16):
        pl.semaphore_signal(barrier, inc=1, device_id=column_device((a + k) % 16, b), device_id_type=MESH)
    for k in range(1, 8):
        pl.semaphore_signal(barrier, inc=1, device_id=column_device(a, (b + k) % 8), device_id_type=MESH)
    loads = [pltpu.make_async_copy(src, dst, in_sem.at[n]) for n, (src, dst) in enumerate(
        ((spin_hbm, spin_v), (acts_hbm, acts_v), (cot_hbm, cot_v), (embed_hbm, embed_v), (slot_hbm, slot_ref)))]
    for copy in loads:
        copy.start()
    for copy in loads:
        copy.wait()
    prepare(spin_v, acts_v, cot_v, embed_v, energy_ref, stage, cstage, lin_ref, cin_ref)
    pl.semaphore_wait(barrier, 22)

    sends = []

    def start(copy):
        copy.start()
        sends.append(copy)

    def arrived(ref, sem):
        remote(ref, ref, sem, sem, partner).wait_recv()

    for k in range(1, 8):
        bt = (b + k) % 8
        start(remote(cin_ref.at[bt], call.at[a, b], c1s.at[k], c1r.at[b], column_device(a, bt)))
    for k in range(1, 16):
        at = (a + k) % 16
        start(remote(lin_ref.at[pl.ds(pl.multiple_of(at * IB, IB), IB)], lraw.at[a], l1s.at[k], l1r.at[a], column_device(at, b)))
    call[a, b] = cin_ref[b]
    lraw[a] = lin_ref[pl.ds(pl.multiple_of(a * IB, IB), IB), :]

    def chalf(p, h):
        return call.at[p] if h is None else call.at[p, pl.ds(4 * h, 4)]

    def lhalf(p, h):
        return lpk.at[p] if h is None else lpk.at[p, pl.ds(5 * h, 5 - h)]

    slot_c, slot_l = [0], [0]

    def csend(org, h, to, seen):
        ref = chalf(cpos(*org), h)
        start(remote(ref, ref, c2s.at[slot_c[0]], c2r.at[seen[0] * 4 + seen[1], h or 0], column_device(cpos(*to), b)))
        slot_c[0] += 1

    def lsend(org, h, to, seen):
        ref = lhalf(lpos(*org), h)
        start(remote(ref, ref, l2s.at[slot_l[0]], l2r.at[seen[0] * 4 + seen[1], h or 0], column_device(a, lpos(*to))))
        slot_l[0] += 1

    def over(org, h=None):
        ref = chalf(cpos(*org), h)
        n = org[0] * 4 + org[1]
        start(remote(ref, ref, c3s.at[n, h or 0], c3r.at[n, h or 0], partner))

    def cwait(org, h=None):
        arrived(chalf(cpos(*org), h), c2r.at[org[0] * 4 + org[1], h or 0])

    def owait(org, h=None):
        arrived(chalf(cpos(*org, 1), h), c3r.at[org[0] * 4 + org[1], h or 0])

    def lwait(org, h=None):
        arrived(lhalf(lpos(*org), h), l2r.at[org[0] * 4 + org[1], h or 0])

    HERE, PAIR, UP, DOWN = (0, 0), (1, 0), (0, 1), (0, 3)

    for k in range(1, 8):
        bs = (b + 8 - k) % 8
        arrived(call.at[a, bs], c1r.at[bs])
    csend(HERE, None, PAIR, (1, 0))
    csend(HERE, None, UP, (0, 3))
    csend(HERE, None, DOWN, (0, 1))
    over(HERE)

    for k in range(1, 16):
        asrc = (a + 16 - k) % 16
        arrived(lraw.at[asrc], l1r.at[asrc])
    packed = jnp.concatenate([lraw[s][:, :ROWS2] for s in range(16)], axis=1)
    for t in range(9):
        lpk[b, t] = packed[:, t * LANES:(t + 1) * LANES]
    lsend(HERE, None, PAIR, (1, 0))
    lsend(HERE, None, UP, (0, 3))
    lsend(HERE, None, DOWN, (0, 1))

    cwait(PAIR)
    csend(PAIR, None, UP, (1, 3))
    csend(PAIR, None, DOWN, (1, 1))
    over(PAIR)
    lwait(PAIR)
    lsend(PAIR, None, UP, (1, 3))
    lsend(PAIR, None, DOWN, (1, 1))
    for u in range(2):
        cwait((u, 3))
        csend((u, 3), 0, UP, (u, 2))
        over((u, 3))
        cwait((u, 1))
        csend((u, 1), 1, DOWN, (u, 2))
        over((u, 1))
        lwait((u, 3))
        lsend((u, 3), 0, UP, (u, 2))
        lwait((u, 1))
        lsend((u, 1), 1, DOWN, (u, 2))

    lane = lax.broadcasted_iota(jnp.int32, (IB, LANES), 1)
    first = jnp.where(lane < TOKS, 1.0, 0.0)
    second = jnp.where((lane >= TOKS) & (lane < ROWS2), 1.0, 0.0)
    lane1 = lax.broadcasted_iota(jnp.int32, (1, LANES), 1)
    scale = jnp.where(lane1 < JB, 1.0 / math.sqrt(TOKS), 0.0)

    def rows_of(other, rc, lsteps):
        asrc = cpos(*rel(rc), other)
        off = asrc * ROWS2
        t0 = off // LANES
        o = off % LANES
        t1 = jnp.minimum(t0 + 1, 8)
        shift = (LANES - o) % LANES
        for rl in lsteps:
            bs = lpos(*rel(rl))
            lo = pltpu.roll(lpk[bs, t0].astype(F32), shift, 1)
            hi = pltpu.roll(lpk[bs, t1].astype(F32), shift, 1)
            left = jnp.where(lane < LANES - o, lo, hi)
            left = jnp.concatenate([left * first, left * second], axis=0).astype(BF)
            right = call[asrc, bs]
            prod = lax.dot_general(left[:, :ROWS2], right, (((1,), (0,)), ((), ())), preferred_element_type=F32)
            at = asrc * 8 + flip(bs, asrc // 8)
            rbuf[pl.ds(pl.multiple_of(at * 2 * IB, 2 * IB), 2 * IB), :] = (prod * scale).astype(BF).astype(F32)
            esc[pl.ds(at, 1), :] = right.astype(F32)[0:1, :]

    def rows_loop(other, lo, hi, lsteps):
        def body(rc, carry):
            rows_of(other, rc, lsteps)
            return carry
        lax.fori_loop(lo, hi, body, 0)

    rows_loop(0, 0, 6, range(6))
    for org in (HERE, PAIR, DOWN, UP, (1, 3), (1, 1)):
        owait(org)
    rows_loop(1, 0, 6, range(6))
    for u in range(2):
        for h in range(2):
            cwait((u, 2), h)
            over((u, 2), h)
        for h in range(2):
            lwait((u, 2), h)
    for other in range(2):
        rows_loop(other, 0, 6, range(6, 8))
    rows_loop(0, 6, 8, range(8))
    for u in range(2):
        for h in range(2):
            owait((u, 2), h)
    rows_loop(1, 6, 8, range(8))

    parts = esc[...]
    pos = lax.broadcasted_iota(jnp.int32, (LANES, LANES), 0) * 2
    for half in range(2):
        row = jnp.zeros((1, LANES), F32)
        for k in range(2):
            e = parts[:, JB + 3 * k:JB + 3 * k + 1] + parts[:, JB + 3 * k + 1:JB + 3 * k + 2] + parts[:, JB + 3 * k + 2:JB + 3 * k + 3]
            hit = slot_ref[half:half + 1, :] == pos + k
            row = row + jnp.sum(jnp.where(hit, e, 0.0), axis=0, keepdims=True)
        erow_ref[half:half + 1, :] = row

    gacc[...] = jnp.zeros_like(gacc)
    inv_root = 1.0 / math.sqrt(WIDTH * WIDTH)

    def gram_step(m, carry):
        xs = [rbuf[pl.ds(pl.multiple_of(s * IB + m * 8, 8), 8), :] for s in range(SLOTS)]
        sums = xs[:8]
        for s in range(8, SLOTS):
            sums[s % 8] = sums[s % 8] + xs[s]
        while len(sums) > 1:
            sums = [sums[n] + sums[n + 1] for n in range(0, len(sums), 2)]
        mean = sums[0] * (1.0 / SLOTS)
        c = jnp.concatenate([((x - mean) * inv_root)[None] for x in xs], axis=0)
        c = jnp.transpose(c, (1, 0, 2)).astype(BF)
        cen_ref[pl.ds(pl.multiple_of(m * 8, 8), 8)] = c
        c = jnp.concatenate([c[n] for n in range(8)], axis=1)
        gacc[...] += lax.dot_general(c, c, (((1,), (1,)), ((), ())), preferred_element_type=F32)
        return carry

    lax.fori_loop(0, IB // 8, gram_step, 0)

    for t in range(48):
        blk, w = t // 16, t % 16
        r0 = (0, 128, 128)[blk] + 8 * w
        c0 = (0, 0, 128)[blk]
        gp[t // 24, (t % 24) // 3, t % 3] = gacc[r0:r0 + 8, c0:c0 + 128]

    start(remote(gp.at[1 - core], cbuf, a_s, a_r, partner))
    arrived(cbuf, a_r)
    cbuf[...] = cbuf[...] + gp[core]
    for k in range(1, 8):
        bt = (b + k) % 8
        start(remote(cbuf.at[bt], rr.at[b], b_s.at[k], b_r.at[b], column_device(a, bt)))
    rr[b] = cbuf[b]
    for k in range(1, 8):
        bs = (b + 8 - k) % 8
        arrived(rr.at[bs], b_r.at[bs])
    total = rr[0]
    for k in range(1, 8):
        total = total + rr[k]
    s1[...] = total
    chip = x_hi * 4 + z
    cr[chip] = total
    for k in range(1, 8):
        ct = (chip + k) % 8
        start(remote(s1, cr.at[chip], x_s.at[k], x_r.at[chip], column_device((ct // 4) * 8 + core * 4 + ct % 4, b)))
    for k in range(1, 8):
        cs = (chip + 8 - k) % 8
        arrived(cr.at[cs], x_r.at[cs])
    total = cr[0]
    for k in range(1, 8):
        total = total + cr[k]
    s2[...] = total
    gt[core, b] = total
    for k in range(1, 8):
        bt = (b + k) % 8
        start(remote(s2, gt.at[core, b], d_s.at[k], d_r.at[b], column_device(a, bt)))
    start(remote(s2, gt.at[core, b], e_s.at[0], e_r.at[b], partner))
    for k in range(1, 8):
        bs = (b + 8 - k) % 8
        arrived(gt.at[core, bs], d_r.at[bs])
        start(remote(gt.at[core, bs], gt.at[core, bs], e_s.at[k], e_r.at[bs], partner))
    for k in range(8):
        bs = (b + 8 - k) % 8
        arrived(gt.at[1 - core, bs], e_r.at[bs])

    for t in range(48):
        blk, w = t // 16, t % 16
        r0 = (0, 128, 128)[blk] + 8 * w
        c0 = (0, 0, 128)[blk]
        W[r0:r0 + 8, c0:c0 + 128] = gt[t // 24, (t % 24) // 3, t % 3]
    W[0:128, 128:256] = W[128:256, 0:128].T
    e_row = jnp.concatenate([erow_ref[0:1, :], erow_ref[1:2, :]], axis=1)
    sh = e_row - jnp.sum(e_row, axis=1, keepdims=True) * (1.0 / SLOTS)
    rows = lax.broadcasted_iota(jnp.int32, (SLOTS, SLOTS), 0)
    cols = lax.broadcasted_iota(jnp.int32, (SLOTS, SLOTS), 1)
    eye = rows == cols
    W[:, 0:SLOTS] = W[:, 0:SLOTS] + jnp.where(eye, damp_ref[0], 0.0)
    W[:, SLOTS:] = jnp.broadcast_to(jnp.sum(jnp.where(eye, sh, 0.0), axis=1, keepdims=True), (SLOTS, LANES))
    weights, last = sweep(W, SLOTS, 8)
    wv[...] = weights
    wv[SLOTS - 8:, :] = last

    step_scale = -math.sqrt(WIDTH * WIDTH / SLOTS)

    def update_step(r, carry):
        done = []
        for v in range(6):
            c = cen_ref[r * 6 + v].astype(F32)
            done.append(jnp.sum(c * wv[...], axis=0, keepdims=True) * step_scale)
        done.append(jnp.zeros((2, LANES), F32))
        upd[r] = jnp.concatenate(done, axis=0)
        return carry

    lax.fori_loop(0, 8, update_step, 0)
    for k in range(1, 8):
        bt = (b + k) % 8
        start(remote(upd.at[flip(bt, x_hi)], ur.at[b], f_s.at[k], f_r.at[b], column_device(a, bt)))
    ur[b] = upd[rb]
    for copy in sends[:-7]:
        copy.wait_send()
    for k in range(1, 8):
        bs = (b + 8 - k) % 8
        arrived(ur.at[bs], f_r.at[bs])
    whole = jnp.concatenate([ur[n][:, :JB] for n in range(8)], axis=1)
    for i in range(6):
        for v in range(6):
            out_ref[6 * i + v:6 * i + v + 1, :] = whole[i:i + 1, v * LANES:(v + 1) * LANES]
    for copy in sends[-7:]:
        copy.wait_send()


def main_call(energies, damping, spin, acts, cot, embed, slots):
    dma = pltpu.SemaphoreType.DMA
    smem = pl.BlockSpec(memory_space=pltpu.SMEM)
    hbm = pl.BlockSpec(memory_space=pl.ANY)
    return pl.pallas_call(
        main_kernel,
        out_shape=jax.ShapeDtypeStruct((36, LANES), F32),
        in_specs=[smem, smem, hbm, hbm, hbm, hbm, hbm],
        out_specs=pl.BlockSpec(memory_space=pltpu.VMEM),
        scratch_shapes=[
            pltpu.VMEM(spin.shape, jnp.int32),
            pltpu.VMEM(acts.shape, BF),
            pltpu.VMEM(cot.shape, BF),
            pltpu.VMEM(embed.shape, BF),
            pltpu.VMEM(slots.shape, jnp.int32),
            dma((5,)),
            pltpu.VMEM((LANES, WIDTH), F32),
            pltpu.VMEM((8, ROWS2, LANES), F32),
            pltpu.VMEM((WIDTH, LANES), BF),
            pltpu.VMEM((8, ROWS2, LANES), BF),
            pltpu.VMEM((2, 8, 3, 8, LANES), F32),
            pltpu.VMEM((2, LANES), F32),
            pltpu.VMEM((IB, SLOTS, LANES), BF),
            pltpu.VMEM((SLOTS, SLOTS + LANES), F32),
            pltpu.VMEM((SLOTS, LANES), F32),
            pltpu.VMEM((8, 8, LANES), F32),
            pltpu.VMEM((8, 8, LANES), F32),
            dma((8,)), dma((8,)),
            pltpu.VMEM((16, IB, LANES), BF),
            pltpu.VMEM((8, 9, IB, LANES), BF),
            pltpu.VMEM((16, 8, ROWS2, LANES), BF),
            pltpu.VMEM((SLOTS * IB, LANES), F32),
            pltpu.VMEM((LANES, LANES), F32),
            pltpu.VMEM((SLOTS, SLOTS), F32),
            pltpu.VMEM((2, 8, 3, 8, LANES), F32),
            pltpu.VMEM((8, 3, 8, LANES), F32),
            pltpu.VMEM((8, 3, 8, LANES), F32),
            pltpu.VMEM((3, 8, LANES), F32),
            pltpu.VMEM((8, 3, 8, LANES), F32),
            pltpu.VMEM((3, 8, LANES), F32),
            dma((16,)), dma((16,)), dma((8,)), dma((8,)), dma((9,)), dma((8, 2)),
            dma((8, 2)), dma((8, 2)), dma((9,)), dma((8, 2)),
            dma(()), dma(()), dma((8,)), dma((8,)), dma((8,)), dma((8,)), dma((8,)), dma((8,)), dma((8,)), dma((8,)),
        ],
        compiler_params=pltpu.CompilerParams(
            collective_id=0, has_side_effects=True, vmem_limit_bytes=48 * 1024 * 1024),
        name="main",
    )(energies, damping, spin, acts, cot, embed, slots)


def shards(spin_config, layer_acts, cotangent, patch_embed, energies, slot_sample, damping):
    out = main_call(energies, damping.reshape(1), spin_config, layer_acts, cotangent, patch_embed,
                    slot_sample.reshape(2, LANES))
    return out.reshape(-1)


def solution(mesh):
    return jax.shard_map(
        shards,
        mesh=mesh,
        in_specs=(
            P(("grp", "dev"), None),
            P(("grp", "dev"), None, None),
            P(("grp", "dev"), None, None),
            P(),
            P(("grp", "dev")),
            P(),
            P(),
        ),
        out_specs=P(("grp", "dev")),
        check_vma=False,
    )
```

time: 77.9 us -> 67.8 us (0.87)
  Pallas kernels: 69.2 us -> 64.6 us
  local copies, waits for them, and re-layouts: 5.21 us -> 2.23 us
  other arithmetic: 1.42 us -> 0 us
  matrix products: 1.05 us -> 0 us
    pallas_call x3 -> x1, Pallas kernels: 69.2 us -> 64.6 us  [main_call(): pl.pallas_call(main_kernel, out_shape=jax.ShapeDtypeStruct((36, LANES), F...]
    unnamed x12 -> x13, local copies, waits for them, and re-layouts: 3.88 us -> 2.23 us
    dot_general x1 -> x0, matrix products: 1.05 us -> none  [shards(): embedded = jnp.einsum('stk,kd->std', patches, patch_embed.astype(F32))]
    reshape x4 -> x0, local copies, waits for them, and re-layouts: 0.9 us -> none  [the longest x1 0.68 us: shards(): return pieces[:, :6, :JB].transpose(1, 0, 2).reshape(-1)]
where the time goes in v4:
time: 67.8 us; the launch traced here: 67.6 us
  Pallas kernels  64.6 us (95%)
  local copies, waits for them, and re-layouts  2.23 us (3%)
  between operations  0.72 us (1%)
    pallas_call x1, Pallas kernels, main_call(): pl.pallas_call(main_kernel, out_shape=jax.ShapeDtypeStruct((36, LANES), F...  64.6 us
    unnamed x13, local copies, waits for them, and re-layouts  2.23 us

profile of v4, /device:TPU:1, one launch (start us, length us, event | category | flops | bytes accessed | tf_op | source)
XLA Modules:
  0.0 67.6 jit_solution(498601910977658550)
XLA Ops:
  0.7 0.0 copy-start.4
  0.7 0.9 %copy.8.acts_hbm = bf16[2,36,768]{2,1,0:T(8,128)(2,1)S(1)} copy(bf16[2,36,768]{2,0,1:T(2,128)(2,1)} %param.8) | data formatting | bytes 221184 | tf_op args[1]
  1.6 0.0 copy-done.4
  1.6 0.0 copy-start
  1.6 0.0 copy-start.1
  1.6 0.0 copy-start.2
  1.7 0.0 copy-start.3
  1.7 0.6 copy-done
  2.3 0.0 copy-done.1
  2.3 0.0 copy-done.2
  2.3 0.0 copy-done.3
  2.3 64.6 %main.1 = f32[36,128]{1,0:T(8,128)S(1)} custom-call(f32[2]{0:T(128)S(1)} %copy-done.3, f32[1]{0:T(128)} %bitcast.3.damp_ref, s32[2,144]{1,0:T(2,128)S(1)} %copy-done.1, bf16[2,36,768]{2,1,0:T(8,128)(2,1)S(1)} %copy.8.acts_hbm, bf16[2,36,768]{2,1,0:T(8,128)(2,1)S(1)} %copy.9.cot_hbm, bf16[4,768]{1,0:T(4,128)(2,1)S(1)} %copy-done, s32[2,128]{1,0:T(2,128)S(1)} %bitcast.5), custom_call_target="tpu_custom_call" | custom-call | tf_op jit(solution)/shard_map/main/pallas_call | solution.py:463
  67.0 0.6 copy.12
  (1 shorter events, 0.0 us)
Async XLA Ops:
  0.7 1.0 %copy-start.4 = (bf16[2,36,768]{2,0,1:T(2,128)(2,1)S(1)}, bf16[2,36,768]{2,0,1:T(2,128)(2,1)}, u32[]{:S(2)}) copy-start(bf16[2,36,768]{2,0,1:T(2,128)(2,1)} %param.9) | copy-start | bytes 331780
  1.6 0.7 %copy-start = (bf16[4,768]{1,0:T(4,128)(2,1)S(1)}, bf16[4,768]{1,0:T(4,128)(2,1)}, u32[]{:S(2)}) copy-start(bf16[4,768]{1,0:T(4,128)(2,1)} %embed_hbm.1) | copy-start | bytes 18436
  1.6 0.7 %copy-start.1 = (s32[2,144]{1,0:T(2,128)S(1)}, s32[2,144]{1,0:T(2,128)}, u32[]{:S(2)}) copy-start(s32[2,144]{1,0:T(2,128)} %spin_hbm.1) | copy-start | bytes 3460
  1.6 0.7 %copy-start.2 = (s32[256]{0:T(256)S(1)}, s32[256]{0:T(256)}, u32[]{:S(2)}) copy-start(s32[256]{0:T(256)} %param.12) | copy-start | bytes 3076
  1.7 0.7 %copy-start.3 = (f32[2]{0:T(128)S(1)}, f32[2]{0:T(128)}, u32[]{:S(2)}) copy-start(f32[2]{0:T(128)} %energy_ref.1) | copy-start | bytes 28

commit v5 on v4

--- a/solution.py
+++ b/solution.py
@@ -128,40 +128,40 @@
 
 
 def prepare(spin, acts, cot, embed, energy_ref, stage, cstage, lin, cin):
-    sub = lax.broadcasted_iota(jnp.int32, (40, SITES), 0)
-    site = lax.broadcasted_iota(jnp.int32, (40, SITES), 1)
+    for t in range(TOKS):
+        stage[2 * t:2 * t + 2, :] = acts[t].astype(F32)
+        cstage[2 * t:2 * t + 2, :] = cot[t].astype(F32)
+    sub = lax.broadcasted_iota(jnp.int32, (ROWS2, SITES), 0)
+    site = lax.broadcasted_iota(jnp.int32, (ROWS2, SITES), 1)
     spins = spin[...].astype(F32)
-    patches = jnp.concatenate(
-        [jnp.where(site // PATCH == sub, spins[s:s + 1, :], 0.0) for s in range(2)], axis=0).astype(BF)
+    patches = jnp.where(sub % 2 == 0, spins[0:1, :], spins[1:2, :])
+    patches = jnp.where(site // PATCH == sub // 2, patches, 0.0).astype(BF)
     turn = lax.broadcasted_iota(jnp.int32, (SITES, WIDTH), 0) % PATCH
     table = embed[...].astype(F32)
     spread = jnp.zeros((SITES, WIDTH), F32)
     for k in range(PATCH):
         spread = jnp.where(turn == k, table[k:k + 1, :], spread)
     added = jnp.dot(patches, spread.astype(BF), preferred_element_type=F32)
-    for s in range(2):
-        stage[TOKS * s:TOKS * (s + 1), :] = (acts[s].astype(F32) + added[40 * s:40 * s + TOKS, :]).astype(BF).astype(F32)
+    stage[:ROWS2, :] = (stage[:ROWS2, :] + added).astype(BF).astype(F32)
     stage[ROWS2:, :] = jnp.zeros((LANES - ROWS2, WIDTH), F32)
     for v in range(WIDTH // LANES):
         lin[v * LANES:(v + 1) * LANES, :] = stage[:, v * LANES:(v + 1) * LANES].T.astype(BF)
-    lane = lax.broadcasted_iota(jnp.int32, (TOKS, LANES), 1)
-    row = lax.broadcasted_iota(jnp.int32, (TOKS, LANES), 0)
-    high, mid, low = (t.astype(F32) for t in split3(
-        jnp.where(lane < JB + 3, jnp.full((TOKS, LANES), energy_ref[0], F32), jnp.full((TOKS, LANES), energy_ref[1], F32))))
+    lane = lax.broadcasted_iota(jnp.int32, (ROWS2, LANES), 1)
+    row = lax.broadcasted_iota(jnp.int32, (ROWS2, LANES), 0)
+    energy = jnp.where(lane < JB + 3, jnp.full((ROWS2, LANES), energy_ref[0], F32), jnp.full((ROWS2, LANES), energy_ref[1], F32))
+    high, mid, low = (t.astype(F32) for t in split3(energy))
     third = lane % 3
     parts = jnp.where(third == 0, high, jnp.where(third == 1, mid, low))
     parts = jnp.where((row == 0) & (lane < JB + 6), parts, 0.0)
-    for s in range(2):
-        x = cot[s].astype(F32)
-        for b in range(8):
-            t, o = (JB * b) // LANES, (JB * b) % LANES
-            piece = x[:, t * LANES:(t + 1) * LANES]
-            if o:
-                piece = pltpu.roll(piece, LANES - o, 1)
-                if LANES - o < JB:
-                    piece = jnp.where(lane < LANES - o, piece, pltpu.roll(x[:, (t + 1) * LANES:(t + 2) * LANES], LANES - o, 1))
-            cstage[b, TOKS * s:TOKS * (s + 1), :] = jnp.where(lane < JB, piece, parts if s == 0 else 0.0)
-    cin[...] = cstage[...].astype(BF)
+    for b in range(8):
+        t, o = (JB * b) // LANES, (JB * b) % LANES
+        piece = cstage[:, t * LANES:(t + 1) * LANES]
+        if o:
+            piece = pltpu.roll(piece, LANES - o, 1)
+            if LANES - o < JB:
+                after = pltpu.roll(cstage[:, (t + 1) * LANES:(t + 2) * LANES], LANES - o, 1)
+                piece = jnp.where(lane < LANES - o, piece, after)
+        cin[b] = jnp.where(lane < JB, piece, parts).astype(BF)
 
 
 def main_kernel(energy_ref, damp_ref, spin_hbm, acts_hbm, cot_hbm, embed_hbm, slot_hbm, out_ref,
@@ -206,11 +206,12 @@
     def arrived(ref, sem):
         remote(ref, ref, sem, sem, partner).wait_recv()
 
-    for k in range(1, 8):
-        bt = (b + k) % 8
+    others = ((1, 2), (0, 2), (1, 1), (1, 3), (0, 1), (0, 3), (1, 0))
+    for k, org in enumerate(others):
+        bt = lpos(*org)
         start(remote(cin_ref.at[bt], call.at[a, b], c1s.at[k], c1r.at[b], column_device(a, bt)))
-    for k in range(1, 16):
-        at = (a + k) % 16
+    for k, (org, other) in enumerate([(org, other) for org in others for other in range(2)] + [((0, 0), 1)]):
+        at = cpos(*org, other)
         start(remote(lin_ref.at[pl.ds(pl.multiple_of(at * IB, IB), IB)], lraw.at[a], l1s.at[k], l1r.at[a], column_device(at, b)))
     call[a, b] = cin_ref[b]
     lraw[a] = lin_ref[pl.ds(pl.multiple_of(a * IB, IB), IB), :]
@@ -268,27 +269,40 @@
     lsend(HERE, None, DOWN, (0, 1))
 
     cwait(PAIR)
-    csend(PAIR, None, UP, (1, 3))
-    csend(PAIR, None, DOWN, (1, 1))
+    csend(PAIR, 1, UP, (1, 3))
+    csend(PAIR, 1, DOWN, (1, 1))
     over(PAIR)
     lwait(PAIR)
-    lsend(PAIR, None, UP, (1, 3))
-    lsend(PAIR, None, DOWN, (1, 1))
-    for u in range(2):
-        cwait((u, 3))
-        csend((u, 3), 0, UP, (u, 2))
-        over((u, 3))
-        cwait((u, 1))
-        csend((u, 1), 1, DOWN, (u, 2))
-        over((u, 1))
-        lwait((u, 3))
-        lsend((u, 3), 0, UP, (u, 2))
-        lwait((u, 1))
-        lsend((u, 1), 1, DOWN, (u, 2))
+    lsend(PAIR, 1, UP, (1, 3))
+    lsend(PAIR, 1, DOWN, (1, 1))
+    cwait((0, 3))
+    csend((0, 3), 0, UP, (0, 2))
+    csend((0, 3), 0, PAIR, (1, 3))
+    over((0, 3))
+    cwait((0, 1))
+    csend((0, 1), 1, DOWN, (0, 2))
+    csend((0, 1), 0, PAIR, (1, 1))
+    over((0, 1))
+    lwait((0, 3))
+    lsend((0, 3), 0, UP, (0, 2))
+    lsend((0, 3), 0, PAIR, (1, 3))
+    lwait((0, 1))
+    lsend((0, 1), 1, DOWN, (0, 2))
+    lsend((0, 1), 0, PAIR, (1, 1))
+    for org, h, to in (((1, 3), 0, UP), ((1, 1), 1, DOWN)):
+        cwait(org, h)
+        csend(org, h, to, (1, 2))
+        over(org, h)
+        lwait(org, h)
+        lsend(org, h, to, (1, 2))
+    for org, h in (((1, 3), 1), ((1, 1), 0)):
+        cwait(org, h)
+        over(org, h)
+        lwait(org, h)
 
     lane = lax.broadcasted_iota(jnp.int32, (IB, LANES), 1)
-    first = jnp.where(lane < TOKS, 1.0, 0.0)
-    second = jnp.where((lane >= TOKS) & (lane < ROWS2), 1.0, 0.0)
+    first = jnp.where((lane % 2 == 0) & (lane < ROWS2), 1.0, 0.0)
+    second = jnp.where((lane % 2 == 1) & (lane < ROWS2), 1.0, 0.0)
     lane1 = lax.broadcasted_iota(jnp.int32, (1, LANES), 1)
     scale = jnp.where(lane1 < JB, 1.0 / math.sqrt(TOKS), 0.0)
 
@@ -318,8 +332,10 @@
         lax.fori_loop(lo, hi, body, 0)
 
     rows_loop(0, 0, 6, range(6))
-    for org in (HERE, PAIR, DOWN, UP, (1, 3), (1, 1)):
+    for org in (HERE, PAIR, DOWN, UP):
         owait(org)
+    for org, h in (((1, 3), 0), ((1, 1), 1), ((1, 3), 1), ((1, 1), 0)):
+        owait(org, h)
     rows_loop(1, 0, 6, range(6))
     for u in range(2):
         for h in range(2):
@@ -335,16 +351,6 @@
             owait((u, 2), h)
     rows_loop(1, 6, 8, range(8))
 
-    parts = esc[...]
-    pos = lax.broadcasted_iota(jnp.int32, (LANES, LANES), 0) * 2
-    for half in range(2):
-        row = jnp.zeros((1, LANES), F32)
-        for k in range(2):
-            e = parts[:, JB + 3 * k:JB + 3 * k + 1] + parts[:, JB + 3 * k + 1:JB + 3 * k + 2] + parts[:, JB + 3 * k + 2:JB + 3 * k + 3]
-            hit = slot_ref[half:half + 1, :] == pos + k
-            row = row + jnp.sum(jnp.where(hit, e, 0.0), axis=0, keepdims=True)
-        erow_ref[half:half + 1, :] = row
-
     gacc[...] = jnp.zeros_like(gacc)
     inv_root = 1.0 / math.sqrt(WIDTH * WIDTH)
 
@@ -374,10 +380,28 @@
     start(remote(gp.at[1 - core], cbuf, a_s, a_r, partner))
     arrived(cbuf, a_r)
     cbuf[...] = cbuf[...] + gp[core]
-    for k in range(1, 8):
-        bt = (b + k) % 8
+    for k, org in enumerate(others):
+        bt = lpos(*org)
         start(remote(cbuf.at[bt], rr.at[b], b_s.at[k], b_r.at[b], column_device(a, bt)))
     rr[b] = cbuf[b]
+
+    parts = esc[...]
+    pos = lax.broadcasted_iota(jnp.int32, (LANES, LANES), 0) * 2
+    for half in range(2):
+        row = jnp.zeros((1, LANES), F32)
+        for k in range(2):
+            e = parts[:, JB + 3 * k:JB + 3 * k + 1] + parts[:, JB + 3 * k + 1:JB + 3 * k + 2] + parts[:, JB + 3 * k + 2:JB + 3 * k + 3]
+            hit = slot_ref[half:half + 1, :] == pos + k
+            row = row + jnp.sum(jnp.where(hit, e, 0.0), axis=0, keepdims=True)
+        erow_ref[half:half + 1, :] = row
+
+    e_row = jnp.concatenate([erow_ref[0:1, :], erow_ref[1:2, :]], axis=1)
+    sh = e_row - jnp.sum(e_row, axis=1, keepdims=True) * (1.0 / SLOTS)
+    rows = lax.broadcasted_iota(jnp.int32, (SLOTS, SLOTS), 0)
+    cols = lax.broadcasted_iota(jnp.int32, (SLOTS, SLOTS), 1)
+    eye = rows == cols
+    W[:, SLOTS:] = jnp.broadcast_to(jnp.sum(jnp.where(eye, sh, 0.0), axis=1, keepdims=True), (SLOTS, LANES))
+
     for k in range(1, 8):
         bs = (b + 8 - k) % 8
         arrived(rr.at[bs], b_r.at[bs])
@@ -387,9 +411,8 @@
     s1[...] = total
     chip = x_hi * 4 + z
     cr[chip] = total
-    for k in range(1, 8):
-        ct = (chip + k) % 8
-        start(remote(s1, cr.at[chip], x_s.at[k], x_r.at[chip], column_device((ct // 4) * 8 + core * 4 + ct % 4, b)))
+    for k, org in enumerate(others):
+        start(remote(s1, cr.at[chip], x_s.at[k], x_r.at[chip], column_device(cpos(*org), b)))
     for k in range(1, 8):
         cs = (chip + 8 - k) % 8
         arrived(cr.at[cs], x_r.at[cs])
@@ -398,12 +421,11 @@
         total = total + cr[k]
     s2[...] = total
     gt[core, b] = total
-    for k in range(1, 8):
-        bt = (b + k) % 8
-        start(remote(s2, gt.at[core, b], d_s.at[k], d_r.at[b], column_device(a, bt)))
+    for k, org in enumerate(others):
+        start(remote(s2, gt.at[core, b], d_s.at[k], d_r.at[b], column_device(a, lpos(*org))))
     start(remote(s2, gt.at[core, b], e_s.at[0], e_r.at[b], partner))
-    for k in range(1, 8):
-        bs = (b + 8 - k) % 8
+    for k, org in zip(range(1, 8), others[::-1]):
+        bs = lpos(*org)
         arrived(gt.at[core, bs], d_r.at[bs])
         start(remote(gt.at[core, bs], gt.at[core, bs], e_s.at[k], e_r.at[bs], partner))
     for k in range(8):
@@ -416,32 +438,26 @@
         c0 = (0, 0, 128)[blk]
         W[r0:r0 + 8, c0:c0 + 128] = gt[t // 24, (t % 24) // 3, t % 3]
     W[0:128, 128:256] = W[128:256, 0:128].T
-    e_row = jnp.concatenate([erow_ref[0:1, :], erow_ref[1:2, :]], axis=1)
-    sh = e_row - jnp.sum(e_row, axis=1, keepdims=True) * (1.0 / SLOTS)
-    rows = lax.broadcasted_iota(jnp.int32, (SLOTS, SLOTS), 0)
-    cols = lax.broadcasted_iota(jnp.int32, (SLOTS, SLOTS), 1)
-    eye = rows == cols
     W[:, 0:SLOTS] = W[:, 0:SLOTS] + jnp.where(eye, damp_ref[0], 0.0)
-    W[:, SLOTS:] = jnp.broadcast_to(jnp.sum(jnp.where(eye, sh, 0.0), axis=1, keepdims=True), (SLOTS, LANES))
     weights, last = sweep(W, SLOTS, 8)
     wv[...] = weights
     wv[SLOTS - 8:, :] = last
 
     step_scale = -math.sqrt(WIDTH * WIDTH / SLOTS)
 
-    def update_step(r, carry):
+    def update_rows(r):
         done = []
         for v in range(6):
             c = cen_ref[r * 6 + v].astype(F32)
             done.append(jnp.sum(c * wv[...], axis=0, keepdims=True) * step_scale)
         done.append(jnp.zeros((2, LANES), F32))
         upd[r] = jnp.concatenate(done, axis=0)
-        return carry
-
-    lax.fori_loop(0, 8, update_step, 0)
-    for k in range(1, 8):
-        bt = (b + k) % 8
+
+    for k, org in enumerate(others):
+        bt = lpos(*org)
+        update_rows(flip(bt, x_hi))
         start(remote(upd.at[flip(bt, x_hi)], ur.at[b], f_s.at[k], f_r.at[b], column_device(a, bt)))
+    update_rows(rb)
     ur[b] = upd[rb]
     for copy in sends[:-7]:
         copy.wait_send()
@@ -473,7 +489,7 @@
             pltpu.VMEM(slots.shape, jnp.int32),
             dma((5,)),
             pltpu.VMEM((LANES, WIDTH), F32),
-            pltpu.VMEM((8, ROWS2, LANES), F32),
+            pltpu.VMEM((ROWS2, WIDTH), F32),
             pltpu.VMEM((WIDTH, LANES), BF),
             pltpu.VMEM((8, ROWS2, LANES), BF),
             pltpu.VMEM((2, 8, 3, 8, LANES), F32),
@@ -496,18 +512,19 @@
             pltpu.VMEM((3, 8, LANES), F32),
             pltpu.VMEM((8, 3, 8, LANES), F32),
             pltpu.VMEM((3, 8, LANES), F32),
-            dma((16,)), dma((16,)), dma((8,)), dma((8,)), dma((9,)), dma((8, 2)),
-            dma((8, 2)), dma((8, 2)), dma((9,)), dma((8, 2)),
+            dma((16,)), dma((16,)), dma((8,)), dma((8,)), dma((11,)), dma((8, 2)),
+            dma((8, 2)), dma((8, 2)), dma((11,)), dma((8, 2)),
             dma(()), dma(()), dma((8,)), dma((8,)), dma((8,)), dma((8,)), dma((8,)), dma((8,)), dma((8,)), dma((8,)),
         ],
         compiler_params=pltpu.CompilerParams(
-            collective_id=0, has_side_effects=True, vmem_limit_bytes=48 * 1024 * 1024),
+            collective_id=0, has_side_effects=True, vmem_limit_bytes=60000000),
         name="main",
     )(energies, damping, spin, acts, cot, embed, slots)
 
 
 def shards(spin_config, layer_acts, cotangent, patch_embed, energies, slot_sample, damping):
-    out = main_call(energies, damping.reshape(1), spin_config, layer_acts, cotangent, patch_embed,
+    out = main_call(energies, damping.reshape(1), spin_config, layer_acts.transpose(1, 0, 2),
+                    cotangent.transpose(1, 0, 2), patch_embed,
                     slot_sample.reshape(2, LANES))
     return out.reshape(-1)
 

time: 67.8 us -> 65.1 us (0.960)
  Pallas kernels: 64.6 us -> 62.9 us
  local copies, waits for them, and re-layouts: 2.23 us -> 1.34 us
    pallas_call x1, Pallas kernels: 64.6 us -> 62.9 us  [main_call(): pl.pallas_call(main_kernel, out_shape=jax.ShapeDtypeStruct((36, LANES), F...]
    unnamed x13 -> x1, local copies, waits for them, and re-layouts: 2.23 us -> 1.34 us
where the time goes in v5:
time: 65.1 us; the launch traced here: 64.9 us
  Pallas kernels  62.9 us (97%)
  local copies, waits for them, and re-layouts  1.34 us (2%)
  between operations  0.66 us (1%)
    pallas_call x1, Pallas kernels, main_call(): pl.pallas_call(main_kernel, out_shape=jax.ShapeDtypeStruct((36, LANES), F...  62.9 us
    unnamed x1, local copies, waits for them, and re-layouts  1.34 us

profile of v5, /device:TPU:1, one launch (start us, length us, event | category | flops | bytes accessed | tf_op | source)
XLA Modules:
  0.0 64.9 jit_solution(15738001453879136126)
XLA Ops:
  0.7 62.9 %main.1 = f32[36,128]{1,0:T(8,128)} custom-call(f32[2]{0:T(128)} %energy_ref.1, f32[1]{0:T(128)} %bitcast.5.damp_ref, s32[2,144]{1,0:T(2,128)} %spin_hbm.1, bf16[36,2,768]{2,1,0:T(2,128)(2,1)} %bitcast.6, bf16[36,2,768]{2,1,0:T(2,128)(2,1)} %bitcast.7, bf16[4,768]{1,0:T(4,128)(2,1)} %embed_hbm.1, s32[2,128]{1,0:T(2,128)} %bitcast.9), custom_call_target="tpu_custom_call" | custom-call | tf_op jit(solution)/shard_map/main/pallas_call | solution.py:479
  63.6 1.3 %copy.10 = f32[4608]{0:T(1024)} copy(f32[4608]{0:T(1024)} %bitcast.8) | data formatting | bytes 36864

commit v6 on v5

--- a/solution.py
+++ b/solution.py
@@ -167,7 +167,7 @@
 def main_kernel(energy_ref, damp_ref, spin_hbm, acts_hbm, cot_hbm, embed_hbm, slot_hbm, out_ref,
                 spin_v, acts_v, cot_v, embed_v, slot_ref, in_sem, stage, cstage, lin_ref, cin_ref,
                 gt, erow_ref, cen_ref, W, wv, upd, ur, f_s, f_r,
-                lraw, lpk, call, rbuf, esc, gacc, gp, cbuf, rr, s1, cr, s2,
+                lraw, lpk, lall, call, rbuf, esc, gacc, gp, cbuf, rr, s1, cr, s2,
                 l1s, l1r, c1s, c1r, c2s, c2r, c3s, c3r, l2s, l2r,
                 a_s, a_r, b_s, b_r, x_s, x_r, d_s, d_r, e_s, e_r):
     g, d, x_hi, core, z, rb = place()
@@ -188,6 +188,9 @@
         pl.semaphore_signal(barrier, inc=1, device_id=column_device((a + k) % 16, b), device_id_type=MESH)
     for k in range(1, 8):
         pl.semaphore_signal(barrier, inc=1, device_id=column_device(a, (b + k) % 8), device_id_type=MESH)
+    across = (1 - 2 * core) * 4
+    for k in range(1, 8):
+        pl.semaphore_signal(barrier, inc=1, device_id=column_device(a + across, (b + k) % 8), device_id_type=MESH)
     loads = [pltpu.make_async_copy(src, dst, in_sem.at[n]) for n, (src, dst) in enumerate(
         ((spin_hbm, spin_v), (acts_hbm, acts_v), (cot_hbm, cot_v), (embed_hbm, embed_v), (slot_hbm, slot_ref)))]
     for copy in loads:
@@ -195,7 +198,7 @@
     for copy in loads:
         copy.wait()
     prepare(spin_v, acts_v, cot_v, embed_v, energy_ref, stage, cstage, lin_ref, cin_ref)
-    pl.semaphore_wait(barrier, 22)
+    pl.semaphore_wait(barrier, 29)
 
     sends = []
 
@@ -249,6 +252,18 @@
         arrived(lhalf(lpos(*org), h), l2r.at[org[0] * 4 + org[1], h or 0])
 
     HERE, PAIR, UP, DOWN = (0, 0), (1, 0), (0, 1), (0, 3)
+    left_lane = lax.broadcasted_iota(jnp.int32, (IB, LANES), 1)
+
+    def unpack(org):
+        bs = lpos(*org)
+        for n in range(16):
+            t, o = (n * ROWS2) // LANES, (n * ROWS2) % LANES
+            tile = lpk[bs, t].astype(F32)
+            if o:
+                tile = pltpu.roll(tile, LANES - o, 1)
+                if LANES - o < ROWS2:
+                    tile = jnp.where(left_lane < LANES - o, tile, pltpu.roll(lpk[bs, t + 1].astype(F32), LANES - o, 1))
+            lall[bs, n] = tile.astype(BF)
 
     for k in range(1, 8):
         bs = (b + 8 - k) % 8
@@ -275,6 +290,8 @@
     lwait(PAIR)
     lsend(PAIR, 1, UP, (1, 3))
     lsend(PAIR, 1, DOWN, (1, 1))
+    lall[b] = lraw[...]
+    unpack(PAIR)
     cwait((0, 3))
     csend((0, 3), 0, UP, (0, 2))
     csend((0, 3), 0, PAIR, (1, 3))
@@ -289,6 +306,8 @@
     lwait((0, 1))
     lsend((0, 1), 1, DOWN, (0, 2))
     lsend((0, 1), 0, PAIR, (1, 1))
+    unpack((0, 3))
+    unpack((0, 1))
     for org, h, to in (((1, 3), 0, UP), ((1, 1), 1, DOWN)):
         cwait(org, h)
         csend(org, h, to, (1, 2))
@@ -299,26 +318,21 @@
         cwait(org, h)
         over(org, h)
         lwait(org, h)
+    unpack((1, 3))
+    unpack((1, 1))
 
     lane = lax.broadcasted_iota(jnp.int32, (IB, LANES), 1)
-    first = jnp.where((lane % 2 == 0) & (lane < ROWS2), 1.0, 0.0)
-    second = jnp.where((lane % 2 == 1) & (lane < ROWS2), 1.0, 0.0)
+    first = jnp.where((lane % 2 == 0) & (lane < ROWS2), 1.0, 0.0).astype(BF)
+    second = jnp.where((lane % 2 == 1) & (lane < ROWS2), 1.0, 0.0).astype(BF)
     lane1 = lax.broadcasted_iota(jnp.int32, (1, LANES), 1)
     scale = jnp.where(lane1 < JB, 1.0 / math.sqrt(TOKS), 0.0)
 
     def rows_of(other, rc, lsteps):
         asrc = cpos(*rel(rc), other)
-        off = asrc * ROWS2
-        t0 = off // LANES
-        o = off % LANES
-        t1 = jnp.minimum(t0 + 1, 8)
-        shift = (LANES - o) % LANES
         for rl in lsteps:
             bs = lpos(*rel(rl))
-            lo = pltpu.roll(lpk[bs, t0].astype(F32), shift, 1)
-            hi = pltpu.roll(lpk[bs, t1].astype(F32), shift, 1)
-            left = jnp.where(lane < LANES - o, lo, hi)
-            left = jnp.concatenate([left * first, left * second], axis=0).astype(BF)
+            left = lall[bs, asrc]
+            left = jnp.concatenate([left * first, left * second], axis=0)
             right = call[asrc, bs]
             prod = lax.dot_general(left[:, :ROWS2], right, (((1,), (0,)), ((), ())), preferred_element_type=F32)
             at = asrc * 8 + flip(bs, asrc // 8)
@@ -343,6 +357,7 @@
             over((u, 2), h)
         for h in range(2):
             lwait((u, 2), h)
+        unpack((u, 2))
     for other in range(2):
         rows_loop(other, 0, 6, range(6, 8))
     rows_loop(0, 6, 8, range(8))
@@ -423,11 +438,11 @@
     gt[core, b] = total
     for k, org in enumerate(others):
         start(remote(s2, gt.at[core, b], d_s.at[k], d_r.at[b], column_device(a, lpos(*org))))
+        start(remote(s2, gt.at[core, b], e_s.at[k + 1], e_r.at[b], column_device(a + across, lpos(*org))))
     start(remote(s2, gt.at[core, b], e_s.at[0], e_r.at[b], partner))
-    for k, org in zip(range(1, 8), others[::-1]):
-        bs = lpos(*org)
+    for k in range(1, 8):
+        bs = (b + 8 - k) % 8
         arrived(gt.at[core, bs], d_r.at[bs])
-        start(remote(gt.at[core, bs], gt.at[core, bs], e_s.at[k], e_r.at[bs], partner))
     for k in range(8):
         bs = (b + 8 - k) % 8
         arrived(gt.at[1 - core, bs], e_r.at[bs])
@@ -443,13 +458,11 @@
     wv[...] = weights
     wv[SLOTS - 8:, :] = last
 
-    step_scale = -math.sqrt(WIDTH * WIDTH / SLOTS)
-
     def update_rows(r):
         done = []
         for v in range(6):
             c = cen_ref[r * 6 + v].astype(F32)
-            done.append(jnp.sum(c * wv[...], axis=0, keepdims=True) * step_scale)
+            done.append(jnp.sum(c * wv[...], axis=0, keepdims=True))
         done.append(jnp.zeros((2, LANES), F32))
         upd[r] = jnp.concatenate(done, axis=0)
 
@@ -502,6 +515,7 @@
             dma((8,)), dma((8,)),
             pltpu.VMEM((16, IB, LANES), BF),
             pltpu.VMEM((8, 9, IB, LANES), BF),
+            pltpu.VMEM((8, 16, IB, LANES), BF),
             pltpu.VMEM((16, 8, ROWS2, LANES), BF),
             pltpu.VMEM((SLOTS * IB, LANES), F32),
             pltpu.VMEM((LANES, LANES), F32),
@@ -526,7 +540,7 @@
     out = main_call(energies, damping.reshape(1), spin_config, layer_acts.transpose(1, 0, 2),
                     cotangent.transpose(1, 0, 2), patch_embed,
                     slot_sample.reshape(2, LANES))
-    return out.reshape(-1)
+    return (out * -math.sqrt(WIDTH * WIDTH / SLOTS)).reshape(-1)
 
 
 def solution(mesh):

time: 65.1 us -> 63.4 us (0.974)
  Pallas kernels: 62.9 us -> 61.2 us
  other arithmetic: 0 us -> 1.34 us
  local copies, waits for them, and re-layouts: 1.34 us -> 0 us
    pallas_call x1, Pallas kernels: 62.9 us -> 61.2 us  [main_call(): pl.pallas_call(main_kernel, out_shape=jax.ShapeDtypeStruct((36, LANES), F...]
    reshape x0 -> x1, other arithmetic: none -> 1.34 us  [shards(): return (out * -math.sqrt(WIDTH * WIDTH / SLOTS)).reshape(-1)]
    unnamed x1 -> x0, local copies, waits for them, and re-layouts: 1.34 us -> none
where the time goes in v6:
time: 63.4 us; the launch traced here: 63.2 us
  Pallas kernels  61.2 us (97%)
  other arithmetic  1.34 us (2%)
  between operations  0.66 us (1%)
    pallas_call x1, Pallas kernels, main_call(): pl.pallas_call(main_kernel, out_shape=jax.ShapeDtypeStruct((36, LANES), F...  61.2 us
    reshape x1, other arithmetic, shards(): return (out * -math.sqrt(WIDTH * WIDTH / SLOTS)).reshape(-1)  1.34 us

profile of v6, /device:TPU:1, one launch (start us, length us, event | category | flops | bytes accessed | tf_op | source)
XLA Modules:
  0.0 63.2 jit_solution(17275265525461309789)
XLA Ops:
  0.7 61.2 %main.1 = f32[36,128]{1,0:T(8,128)} custom-call(f32[2]{0:T(128)} %energy_ref.1, f32[1]{0:T(128)} %bitcast.6.damp_ref, s32[2,144]{1,0:T(2,128)} %spin_hbm.1, bf16[36,2,768]{2,1,0:T(2,128)(2,1)} %bitcast.7, bf16[36,2,768]{2,1,0:T(2,128)(2,1)} %bitcast.8, bf16[4,768]{1,0:T(4,128)(2,1)} %embed_hbm.1, s32[2,128]{1,0:T(2,128)} %bitcast.9), custom_call_target="tpu_custom_call" | custom-call | tf_op jit(solution)/shard_map/main/pallas_call | solution.py:492
  61.9 1.3 %multiply_bitcast_fusion = f32[4608]{0:T(1024)} fusion(f32[36,128]{1,0:T(8,128)} %main.1), kind=kLoop, calls=%fused_computation | loop fusion | flops 4608 | bytes 36864 | tf_op jit(solution)/shard_map/reshape | solution.py:543

commit v7 on v6

--- a/solution.py
+++ b/solution.py
@@ -89,10 +89,9 @@
             dinv = jnp.where(lane == l0 + j, c[j], dinv)
         inside = (lane >= l0) & (lane < l0 + B)
         ident = jnp.where(lane == l0 + sub, 1.0, 0.0)
-        x, xs = list(p), list(p)
+        x = list(p)
         x[t0] = jnp.where(inside, ident - dinv, p[t0])
-        xs[t0] = jnp.where(inside, -dinv, p[t0])
-        return x, xs
+        return x, p[T]
 
     def stack(p, x):
         ph, pm, pl_ = split3(p)
@@ -108,8 +107,13 @@
         if old is not None:
             po, xo, xso = old
             ps, xs = stack(cat(po[:T]), cat(xo))
-            W[...] = W[...] - lax.dot_general(ps, xs, tn, preferred_element_type=F32)
-            W[B * (k - 1):B * k, :] = cat(xso)
+            r0 = B * (k + 1)
+            m0 = LANES if r0 >= LANES else 0
+            if r0 < n:
+                change = lax.dot_general(ps[:, m0:], xs[:, :n], tn, preferred_element_type=F32)
+                W[r0:, :n] = W[r0:, :n] - change[r0 - m0:, :]
+            W[:, n:] = W[:, n:] - lax.dot_general(ps, xs[:, n:], tn, preferred_element_type=F32)
+            W[B * (k - 1):B * k, n:] = xso
         x, xs = chain(k, p)
         old = (p, x, xs)
         if k + 1 < n // B:
@@ -124,7 +128,7 @@
             p = nxt
     po, xo, xso = old
     ps, xs = stack(cat(po[:T]), xo[T])
-    return W[:, n:] - lax.dot_general(ps, xs, tn, preferred_element_type=F32), xso[T]
+    return W[:, n:] - lax.dot_general(ps, xs, tn, preferred_element_type=F32), xso
 
 
 def prepare(spin, acts, cot, embed, energy_ref, stage, cstage, lin, cin):

time: 63.4 us -> 62.7 us (0.989)
  Pallas kernels: 61.2 us -> 60.5 us
    pallas_call x1, Pallas kernels: 61.2 us -> 60.5 us  [main_call(): pl.pallas_call(main_kernel, out_shape=jax.ShapeDtypeStruct((36, LANES), F...]
where the time goes in v7:
time: 62.7 us; the launch traced here: 62.5 us
  Pallas kernels  60.5 us (96%)
  other arithmetic  1.34 us (2%)
  between operations  0.66 us (1%)
    pallas_call x1, Pallas kernels, main_call(): pl.pallas_call(main_kernel, out_shape=jax.ShapeDtypeStruct((36, LANES), F...  60.5 us
    reshape x1, other arithmetic, shards(): return (out * -math.sqrt(WIDTH * WIDTH / SLOTS)).reshape(-1)  1.34 us

profile of v7, /device:TPU:1, one launch (start us, length us, event | category | flops | bytes accessed | tf_op | source)
XLA Modules:
  0.0 62.5 jit_solution(4258471627840251289)
XLA Ops:
  0.7 60.5 %main.1 = f32[36,128]{1,0:T(8,128)} custom-call(f32[2]{0:T(128)} %energy_ref.1, f32[1]{0:T(128)} %bitcast.6.damp_ref, s32[2,144]{1,0:T(2,128)} %spin_hbm.1, bf16[36,2,768]{2,1,0:T(2,128)(2,1)} %bitcast.7, bf16[36,2,768]{2,1,0:T(2,128)(2,1)} %bitcast.8, bf16[4,768]{1,0:T(4,128)(2,1)} %embed_hbm.1, s32[2,128]{1,0:T(2,128)} %bitcast.9), custom_call_target="tpu_custom_call" | custom-call | tf_op jit(solution)/shard_map/main/pallas_call | solution.py:496
  61.2 1.3 %multiply_bitcast_fusion = f32[4608]{0:T(1024)} fusion(f32[36,128]{1,0:T(8,128)} %main.1), kind=kLoop, calls=%fused_computation | loop fusion | flops 4608 | bytes 36864 | tf_op jit(solution)/shard_map/reshape | solution.py:547

commit v8 on v7

--- a/solution.py
+++ b/solution.py
@@ -347,7 +347,7 @@
         def body(rc, carry):
             rows_of(other, rc, lsteps)
             return carry
-        lax.fori_loop(lo, hi, body, 0)
+        lax.fori_loop(lo, hi, body, 0, unroll=2)
 
     rows_loop(0, 0, 6, range(6))
     for org in (HERE, PAIR, DOWN, UP):
@@ -388,7 +388,7 @@
         gacc[...] += lax.dot_general(c, c, (((1,), (1,)), ((), ())), preferred_element_type=F32)
         return carry
 
-    lax.fori_loop(0, IB // 8, gram_step, 0)
+    lax.fori_loop(0, IB // 8, gram_step, 0, unroll=2)
 
     for t in range(48):
         blk, w = t // 16, t % 16

time: 62.7 us -> 61.5 us (0.981)
  Pallas kernels: 60.5 us -> 59.3 us
    pallas_call x1, Pallas kernels: 60.5 us -> 59.3 us  [main_call(): pl.pallas_call(main_kernel, out_shape=jax.ShapeDtypeStruct((36, LANES), F...]
where the time goes in v8:
time: 61.5 us; the launch traced here: 61.3 us
  Pallas kernels  59.3 us (96%)
  other arithmetic  1.34 us (2%)
  between operations  0.66 us (1%)
    pallas_call x1, Pallas kernels, main_call(): pl.pallas_call(main_kernel, out_shape=jax.ShapeDtypeStruct((36, LANES), F...  59.3 us
    reshape x1, other arithmetic, shards(): return (out * -math.sqrt(WIDTH * WIDTH / SLOTS)).reshape(-1)  1.34 us

profile of v8, /device:TPU:1, one launch (start us, length us, event | category | flops | bytes accessed | tf_op | source)
XLA Modules:
  0.0 61.3 jit_solution(17002093422167552607)
XLA Ops:
  0.7 59.3 %main.1 = f32[36,128]{1,0:T(8,128)} custom-call(f32[2]{0:T(128)} %energy_ref.1, f32[1]{0:T(128)} %bitcast.6.damp_ref, s32[2,144]{1,0:T(2,128)} %spin_hbm.1, bf16[36,2,768]{2,1,0:T(2,128)(2,1)} %bitcast.7, bf16[36,2,768]{2,1,0:T(2,128)(2,1)} %bitcast.8, bf16[4,768]{1,0:T(4,128)(2,1)} %embed_hbm.1, s32[2,128]{1,0:T(2,128)} %bitcast.9), custom_call_target="tpu_custom_call" | custom-call | tf_op jit(solution)/shard_map/main/pallas_call | solution.py:496
  59.9 1.3 %multiply_bitcast_fusion = f32[4608]{0:T(1024)} fusion(f32[36,128]{1,0:T(8,128)} %main.1), kind=kLoop, calls=%fused_computation | loop fusion | flops 4608 | bytes 36864 | tf_op jit(solution)/shard_map/reshape | solution.py:547
